TPU v7x, 128 devices: a whole 4x4x4 slice. The times are simulated.
128 devices in a mesh: rep: 4 (over y), seq: 32 (over x, z, core).
Axes of the slice: x: 4, y: 4, z: 4, core: 2. Of those that a mesh axis runs over, the one named last changes fastest.
Arguments:
- query: bfloat16 [20480, 4096], P(('rep', 'seq')), parts along dimension 0, may hold values from -320 to 320
- key: bfloat16 [20480, 4096], P(('rep', 'seq')), parts along dimension 0, may hold values from -6 to 6
- value: bfloat16 [20480, 4096], P(('rep', 'seq')), parts along dimension 0, may hold values from -6 to 6
- latent: bfloat16 [16, 128, 640], P('rep', 'seq'), parts along dimension 0, may hold values from -6 to 6
- band_rows: int32 [128], P('rep'), parts along dimension 0, may hold values from 2 to 6, as said below
- head_weight: bfloat16 [4096, 64], replicated, may hold values from -1.1953125 to 1.1953125
- conv_in: bfloat16 [3, 3, 3, 16, 384], replicated, may hold values from -0.3125 to 0.3125
- conv_mid: bfloat16 [3, 3, 3, 384, 384], replicated, may hold values from -0.0625 to 0.0625
- gamma: float32 [384], replicated, may hold values from 0.25 to 1.75
Outputs:
- frames_out: bfloat16 [16, 192, 40, 384], P('rep', 'seq'), parts along dimension 0
There are 4 independent parts, one for each index of `rep`. A program takes and returns all parts, laid end to end along the dimension named above; an argument that names none is the same for every part. Nothing has to cross between parts.
Inputs may be any that keep to these rules, and one draw needn't show every extreme that they name: `band_rows`: devices come in pairs 2p, 2p+1 whose counts are 4 + s and 4 - s with s from 0 to 2; some pair has s = 2.
All inputs are finite; a program needn't handle non-finite values.
Results may differ from a plain program's by a relative error of at most 0.018.
Values may be sent and summed in bfloat16 or wider, within the bound.
A program may use at most 64 MiB of HBM per device.

v0:
```python
import math

import jax
import jax.numpy as jnp
from jax import lax
from jax.sharding import PartitionSpec as P

HEADS = 32
HEAD = 128
LAT_CH = 16
FRAMES = 4
BAND = 2
PCOLS = 20


def with_halo(cells, sides, width):
    for axis, dim in sides:
        count = lax.axis_size(axis)
        ends = count - 1
        head = lax.slice_in_dim(cells, 0, width, axis=dim)
        tail = lax.slice_in_dim(cells, cells.shape[dim] - width, cells.shape[dim], axis=dim)
        cells = jnp.concatenate(
            [
                lax.ppermute(tail, axis, [(i, (i + 1) % count) for i in range(ends)]),
                cells,
                lax.ppermute(head, axis, [((i + 1) % count, i) for i in range(ends)]),
            ],
            axis=dim,
        )
    return cells


def causal_conv(field, weight):
    padded = jnp.pad(field, ((2, 0), (0, 0), (1, 1), (0, 0)))
    return lax.conv_general_dilated(
        padded[None],
        weight,
        (1, 1, 1),
        "VALID",
        dimension_numbers=("NDHWC", "DHWIO", "NDHWC"),
        preferred_element_type=jnp.float32,
    )[0]


def decode_rows(window, first_row, total_rows, conv_in, conv_mid, gamma):
    first_conv = causal_conv(window, conv_in).astype(jnp.bfloat16)
    values32 = first_conv.astype(jnp.float32)
    row_ids = first_row + 1 + jnp.arange(first_conv.shape[1], dtype=jnp.int32)
    inside = (row_ids >= 0) & (row_ids < total_rows)
    normed = (
        values32 * lax.rsqrt(jnp.mean(values32 * values32, axis=-1, keepdims=True) + 1e-06) * gamma
    )
    normed = jnp.where(inside[None, :, None, None], jax.nn.silu(normed), 0.0).astype(jnp.bfloat16)
    mid_conv = causal_conv(normed, conv_mid)
    return (values32[:, 1:-1] + mid_conv).astype(jnp.bfloat16)


def attend_block(q_block, key_heads, value_heads, score_scale):
    scores = (
        jnp.einsum("qhd,khd->hqk", q_block, key_heads, preferred_element_type=jnp.float32)
        * score_scale
    )
    peaks = jnp.max(scores, axis=2, keepdims=True)
    weights = jnp.exp(scores - peaks)
    totals = jnp.sum(weights, axis=2)
    result = jnp.einsum(
        "hqk,khd->qhd",
        weights.astype(jnp.bfloat16),
        value_heads,
        preferred_element_type=jnp.float32,
    )
    return (result / totals.T[:, :, None]).astype(jnp.bfloat16)


def head_attention(pieces):
    q_in, k_in, v_in = pieces
    tokens = q_in.shape[0]
    head_count = q_in.shape[2]
    q_heads = q_in[:, 0]
    key_heads = k_in[:, 0]
    value_heads = v_in[:, 0]
    score_scale = 1.0 / math.sqrt(HEAD)
    block_rows = 512
    q_blocks = q_heads.reshape(tokens // block_rows, block_rows, head_count, HEAD)
    result = lax.map(
        lambda block: attend_block(block, key_heads, value_heads, score_scale), q_blocks
    )
    return result.reshape(tokens, 1, head_count, HEAD)


def per_device(query, key, value, latent, band_rows, head_weight, conv_in, conv_mid, gamma):
    tok_dev, qkv_width = query.shape
    groups = lax.axis_size("seq")
    place = lax.axis_index("seq")
    heads_dev = HEADS // groups
    queries = query.reshape(tok_dev, groups, heads_dev, HEAD)
    keys_in = key.reshape(tok_dev, groups, heads_dev, HEAD)
    values_in = value.reshape(tok_dev, groups, heads_dev, HEAD)
    attended = head_attention(
        (
            lax.all_to_all(queries, "seq", split_axis=1, concat_axis=0, tiled=True),
            lax.all_to_all(keys_in, "seq", split_axis=1, concat_axis=0, tiled=True),
            lax.all_to_all(values_in, "seq", split_axis=1, concat_axis=0, tiled=True),
        )
    )
    returned = lax.all_to_all(attended, "seq", split_axis=0, concat_axis=1, tiled=True)
    velocity = jnp.dot(
        returned.reshape(tok_dev, qkv_width), head_weight, preferred_element_type=jnp.float32
    )
    band_len = 2 * BAND
    most_rows = 3 * BAND
    lat_cols = latent.shape[2] // LAT_CH
    grid = velocity.reshape(FRAMES, BAND, PCOLS, 2, 2, LAT_CH).transpose(0, 1, 3, 2, 4, 5)
    grid = grid.reshape(FRAMES, band_len, lat_cols * LAT_CH)
    clean = (latent.astype(jnp.float32) - 0.9 * grid).astype(jnp.bfloat16)
    total_rows = band_len * groups
    device_ids = jnp.arange(groups, dtype=jnp.int32)
    row_start = jnp.sum(jnp.where(device_ids < place, band_rows, 0))
    length = jnp.sum(jnp.where(device_ids == place, band_rows, 0))
    padded = with_halo(clean, (("seq", 1),), band_len)
    offset = jnp.clip(row_start - 2 - place * band_len + band_len, 0, 3 * band_len - most_rows - 4)
    window = lax.dynamic_slice_in_dim(padded, offset, most_rows + 4, 1)
    first_row = place * band_len - band_len + offset
    decoded = decode_rows(
        window.reshape(FRAMES, most_rows + 4, lat_cols, LAT_CH),
        first_row,
        total_rows,
        conv_in,
        conv_mid,
        gamma,
    )
    lead_rows = row_start - first_row - 2
    extended = jnp.concatenate([decoded, jnp.zeros_like(decoded)], axis=1)
    picked = lax.dynamic_slice_in_dim(extended, lead_rows, most_rows, 1)
    keep_mask = jnp.arange(most_rows, dtype=jnp.int32) < length
    return jnp.where(keep_mask[None, :, None, None], picked, jnp.zeros_like(picked))


def solution(mesh):
    return jax.shard_map(
        per_device,
        mesh=mesh,
        in_specs=(
            P(("rep", "seq"), None),
            P(("rep", "seq"), None),
            P(("rep", "seq"), None),
            P("rep", "seq", None),
            P("rep"),
            P(),
            P(),
            P(),
            P(),
        ),
        out_specs=P("rep", "seq", None, None),
        check_vma=False,
    )
```

profile of v0, /device:TPU:0, one launch (start us, length us, event | category | flops | bytes accessed | tf_op | source)
XLA Modules:
  0.0 223.4 jit_solution(16322020084166523118)
XLA Ops:
  0.0 1.7 copy.81
  3.2 8.4 %all-to-all-start = ((bf16[160,32,1,128]{3,0,2,1:T(8,128)(2,1)}), bf16[160,32,1,128]{3,0,2,1:T(8,128)(2,1)S(1)}, u32[]{:S(2)}, u32[]{:S(2)}) async-start(bf16[160,32,1,128]{3,0,2,1:T(8,128)(2,1)} %copy.58), calls=%async_computation | async-start | bytes 2621440 | tf_op jit(solution)/shard_map/all_to_all | solution.py:101
  11.9 1.6 copy.59
  13.5 18.1 %all-to-all-done = bf16[160,32,1,128]{3,0,2,1:T(8,128)(2,1)S(1)} async-done(((bf16[160,32,1,128]{3,0,2,1:T(8,128)(2,1)}), bf16[160,32,1,128]{3,0,2,1:T(8,128)(2,1)S(1)}, u32[]{:S(2)}, u32[]{:S(2)}) %all-to-all-start) | async-done | bytes 1310752 | tf_op jit(solution)/shard_map/all_to_all | solution.py:101
  31.6 4.0 %all-to-all-start.1 = ((bf16[160,32,1,128]{3,0,2,1:T(8,128)(2,1)}), bf16[160,32,1,128]{3,0,2,1:T(8,128)(2,1)S(1)}, u32[]{:S(2)}, u32[]{:S(2)}) async-start(bf16[160,32,1,128]{3,0,2,1:T(8,128)(2,1)} %copy.59), calls=%async_computation.1 | async-start | bytes 2621440 | tf_op jit(solution)/shard_map/all_to_all | solution.py:102
  35.5 1.6 copy.83
  38.7 16.7 %all-to-all-done.1 = bf16[160,32,1,128]{3,0,2,1:T(8,128)(2,1)S(1)} async-done(((bf16[160,32,1,128]{3,0,2,1:T(8,128)(2,1)}), bf16[160,32,1,128]{3,0,2,1:T(8,128)(2,1)S(1)}, u32[]{:S(2)}, u32[]{:S(2)}) %all-to-all-start.1) | async-done | bytes 1310752 | tf_op jit(solution)/shard_map/all_to_all | solution.py:102
  55.5 4.7 %all-to-all-start.2 = ((bf16[160,32,1,128]{3,0,2,1:T(8,128)(2,1)}), bf16[160,32,1,128]{3,0,2,1:T(8,128)(2,1)}, u32[]{:S(2)}, u32[]{:S(2)}) async-start(bf16[160,32,1,128]{3,0,2,1:T(8,128)(2,1)} %copy.60), calls=%async_computation.2 | async-start | bytes 2621440 | tf_op jit(solution)/shard_map/all_to_all | solution.py:103
  60.2 19.9 %all-to-all-done.2 = bf16[160,32,1,128]{3,0,2,1:T(8,128)(2,1)} async-done(((bf16[160,32,1,128]{3,0,2,1:T(8,128)(2,1)}), bf16[160,32,1,128]{3,0,2,1:T(8,128)(2,1)}, u32[]{:S(2)}, u32[]{:S(2)}) %all-to-all-start.2) | async-done | bytes 1310752 | tf_op jit(solution)/shard_map/all_to_all | solution.py:103
  80.1 72.4 %while.10 = (s32[]{:T(128)}, bf16[10,512,1,128]{3,1,2,0:T(8,128)(2,1)}, bf16[10,512,1,128]{3,1,2,0:T(8,128)(2,1)S(1)}, bf16[5120,1,128]{2,0,1:T(8,128)(2,1)S(1)}, bf16[5120,1,128]{2,0,1:T(8,128)(2,1)}, /*index=5*/s32[]{:T(128)}) while((s32[]{:T(128)}, bf16[10,512,1,128]{3,1,2,0:T(8,128)(2,1)}, bf16[10,512,1,128]{3,1,2,0:T(8,128)(2,1)S(1)}, ...), condition=%wide.region_4.5_spmd, body=%wide.region_1.4_spmd.sunk | while | flops 1363278848 | bytes 34351688 | solution.py:85
  80.1 1.6 multiply_reduce_fusion.3
  81.7 1.8 fusion.84
  83.5 3.8 %fusion.85 = bf16[10,512,1,128]{3,1,2,0:T(8,128)(2,1)} fusion(bf16[10,512,1,128]{3,1,2,0:T(8,128)(2,1)} %get-tuple-element.109, s32[]{:T(128)} %get-tuple-element.108, bf16[5120,1,128]{2,0,1:T(8,128)(2,1)} %get-tuple-element.118, f32[512,5120]{1,0:T(8,128)S(1)} %get-tuple-element.100, f32[512]{0:T(512)S(1)} %get-tuple-element.101, f32[512]{0:T(512)S(1)} %fusion.84), kind=kOutput, calls=%fused_computation.12.clone.1 | convolution fusion | flops 679084032 | bytes 11932160 | tf_op jit(solution)/shard_map/while/body/eval_jaxpr/hqk,khd->qhd/dot_general | solution.py:66
  87.3 1.6 multiply_reduce_fusion.3
  88.9 1.8 fusion.84
  90.8 3.8 %fusion.85 = bf16[10,512,1,128]{3,1,2,0:T(8,128)(2,1)} fusion(bf16[10,512,1,128]{3,1,2,0:T(8,128)(2,1)} %get-tuple-element.109, s32[]{:T(128)} %get-tuple-element.108, bf16[5120,1,128]{2,0,1:T(8,128)(2,1)} %get-tuple-element.118, f32[512,5120]{1,0:T(8,128)S(1)} %get-tuple-element.100, f32[512]{0:T(512)S(1)} %get-tuple-element.101, f32[512]{0:T(512)S(1)} %fusion.84), kind=kOutput, calls=%fused_computation.12.clone.1 | convolution fusion | flops 679084032 | bytes 11932160 | tf_op jit(solution)/shard_map/while/body/eval_jaxpr/hqk,khd->qhd/dot_general | solution.py:66
  94.6 1.6 multiply_reduce_fusion.3
  96.2 1.8 fusion.84
  98.0 3.8 %fusion.85 = bf16[10,512,1,128]{3,1,2,0:T(8,128)(2,1)} fusion(bf16[10,512,1,128]{3,1,2,0:T(8,128)(2,1)} %get-tuple-element.109, s32[]{:T(128)} %get-tuple-element.108, bf16[5120,1,128]{2,0,1:T(8,128)(2,1)} %get-tuple-element.118, f32[512,5120]{1,0:T(8,128)S(1)} %get-tuple-element.100, f32[512]{0:T(512)S(1)} %get-tuple-element.101, f32[512]{0:T(512)S(1)} %fusion.84), kind=kOutput, calls=%fused_computation.12.clone.1 | convolution fusion | flops 679084032 | bytes 11932160 | tf_op jit(solution)/shard_map/while/body/eval_jaxpr/hqk,khd->qhd/dot_general | solution.py:66
  101.8 1.6 multiply_reduce_fusion.3
  103.4 1.8 fusion.84
  105.3 3.8 %fusion.85 = bf16[10,512,1,128]{3,1,2,0:T(8,128)(2,1)} fusion(bf16[10,512,1,128]{3,1,2,0:T(8,128)(2,1)} %get-tuple-element.109, s32[]{:T(128)} %get-tuple-element.108, bf16[5120,1,128]{2,0,1:T(8,128)(2,1)} %get-tuple-element.118, f32[512,5120]{1,0:T(8,128)S(1)} %get-tuple-element.100, f32[512]{0:T(512)S(1)} %get-tuple-element.101, f32[512]{0:T(512)S(1)} %fusion.84), kind=kOutput, calls=%fused_computation.12.clone.1 | convolution fusion | flops 679084032 | bytes 11932160 | tf_op jit(solution)/shard_map/while/body/eval_jaxpr/hqk,khd->qhd/dot_general | solution.py:66
  109.1 1.6 multiply_reduce_fusion.3
  110.7 1.8 fusion.84
  112.5 3.8 %fusion.85 = bf16[10,512,1,128]{3,1,2,0:T(8,128)(2,1)} fusion(bf16[10,512,1,128]{3,1,2,0:T(8,128)(2,1)} %get-tuple-element.109, s32[]{:T(128)} %get-tuple-element.108, bf16[5120,1,128]{2,0,1:T(8,128)(2,1)} %get-tuple-element.118, f32[512,5120]{1,0:T(8,128)S(1)} %get-tuple-element.100, f32[512]{0:T(512)S(1)} %get-tuple-element.101, f32[512]{0:T(512)S(1)} %fusion.84), kind=kOutput, calls=%fused_computation.12.clone.1 | convolution fusion | flops 679084032 | bytes 11932160 | tf_op jit(solution)/shard_map/while/body/eval_jaxpr/hqk,khd->qhd/dot_general | solution.py:66
  116.3 1.6 multiply_reduce_fusion.3
  117.9 1.8 fusion.84
  119.8 3.8 %fusion.85 = bf16[10,512,1,128]{3,1,2,0:T(8,128)(2,1)} fusion(bf16[10,512,1,128]{3,1,2,0:T(8,128)(2,1)} %get-tuple-element.109, s32[]{:T(128)} %get-tuple-element.108, bf16[5120,1,128]{2,0,1:T(8,128)(2,1)} %get-tuple-element.118, f32[512,5120]{1,0:T(8,128)S(1)} %get-tuple-element.100, f32[512]{0:T(512)S(1)} %get-tuple-element.101, f32[512]{0:T(512)S(1)} %fusion.84), kind=kOutput, calls=%fused_computation.12.clone.1 | convolution fusion | flops 679084032 | bytes 11932160 | tf_op jit(solution)/shard_map/while/body/eval_jaxpr/hqk,khd->qhd/dot_general | solution.py:66
  123.6 1.6 multiply_reduce_fusion.3
  125.2 1.8 fusion.84
  127.0 3.8 %fusion.85 = bf16[10,512,1,128]{3,1,2,0:T(8,128)(2,1)} fusion(bf16[10,512,1,128]{3,1,2,0:T(8,128)(2,1)} %get-tuple-element.109, s32[]{:T(128)} %get-tuple-element.108, bf16[5120,1,128]{2,0,1:T(8,128)(2,1)} %get-tuple-element.118, f32[512,5120]{1,0:T(8,128)S(1)} %get-tuple-element.100, f32[512]{0:T(512)S(1)} %get-tuple-element.101, f32[512]{0:T(512)S(1)} %fusion.84), kind=kOutput, calls=%fused_computation.12.clone.1 | convolution fusion | flops 679084032 | bytes 11932160 | tf_op jit(solution)/shard_map/while/body/eval_jaxpr/hqk,khd->qhd/dot_general | solution.py:66
  130.8 1.6 multiply_reduce_fusion.3
  132.4 1.8 fusion.84
  134.2 3.8 %fusion.85 = bf16[10,512,1,128]{3,1,2,0:T(8,128)(2,1)} fusion(bf16[10,512,1,128]{3,1,2,0:T(8,128)(2,1)} %get-tuple-element.109, s32[]{:T(128)} %get-tuple-element.108, bf16[5120,1,128]{2,0,1:T(8,128)(2,1)} %get-tuple-element.118, f32[512,5120]{1,0:T(8,128)S(1)} %get-tuple-element.100, f32[512]{0:T(512)S(1)} %get-tuple-element.101, f32[512]{0:T(512)S(1)} %fusion.84), kind=kOutput, calls=%fused_computation.12.clone.1 | convolution fusion | flops 679084032 | bytes 11932160 | tf_op jit(solution)/shard_map/while/body/eval_jaxpr/hqk,khd->qhd/dot_general | solution.py:66
  138.0 1.6 multiply_reduce_fusion.3
  139.6 1.8 fusion.84
  141.5 3.8 %fusion.85 = bf16[10,512,1,128]{3,1,2,0:T(8,128)(2,1)} fusion(bf16[10,512,1,128]{3,1,2,0:T(8,128)(2,1)} %get-tuple-element.109, s32[]{:T(128)} %get-tuple-element.108, bf16[5120,1,128]{2,0,1:T(8,128)(2,1)} %get-tuple-element.118, f32[512,5120]{1,0:T(8,128)S(1)} %get-tuple-element.100, f32[512]{0:T(512)S(1)} %get-tuple-element.101, f32[512]{0:T(512)S(1)} %fusion.84), kind=kOutput, calls=%fused_computation.12.clone.1 | convolution fusion | flops 679084032 | bytes 11932160 | tf_op jit(solution)/shard_map/while/body/eval_jaxpr/hqk,khd->qhd/dot_general | solution.py:66
  145.3 1.6 multiply_reduce_fusion.3
  146.9 1.8 fusion.84
  148.7 3.8 %fusion.85 = bf16[10,512,1,128]{3,1,2,0:T(8,128)(2,1)} fusion(bf16[10,512,1,128]{3,1,2,0:T(8,128)(2,1)} %get-tuple-element.109, s32[]{:T(128)} %get-tuple-element.108, bf16[5120,1,128]{2,0,1:T(8,128)(2,1)} %get-tuple-element.118, f32[512,5120]{1,0:T(8,128)S(1)} %get-tuple-element.100, f32[512]{0:T(512)S(1)} %get-tuple-element.101, f32[512]{0:T(512)S(1)} %fusion.84), kind=kOutput, calls=%fused_computation.12.clone.1 | convolution fusion | flops 679084032 | bytes 11932160 | tf_op jit(solution)/shard_map/while/body/eval_jaxpr/hqk,khd->qhd/dot_general | solution.py:66
  153.0 3.0 %reduce.4 = bf16[5120,128]{1,0:T(8,128)(2,1)S(1)} reduce(bf16[5120,1,1,128]{3,0,2,1:T(8,128)(2,1)} %bitcast.17, bf16[]{:T(256)} %broadcast.109), dimensions={1,2}, to_apply=%copy.62.reduce_sub_computation | reduce | bytes 2621442 | tf_op jit(solution)/shard_map/reshape | solution.py:88
  157.2 5.0 %all-to-all-start.3 = ((bf16[32,2,10240]{2,1,0:T(2,128)(2,1)}), bf16[32,2,10240]{2,1,0:T(2,128)(2,1)}, u32[]{:S(2)}, u32[]{:S(2)}) async-start(bf16[32,2,10240]{2,1,0:T(2,128)(2,1)} %reshape.117), calls=%async_computation.3 | async-start | bytes 2621440 | tf_op jit(solution)/shard_map/all_to_all | solution.py:106
  163.7 18.3 %all-to-all-done.3 = bf16[32,2,10240]{2,1,0:T(2,128)(2,1)} async-done(((bf16[32,2,10240]{2,1,0:T(2,128)(2,1)}), bf16[32,2,10240]{2,1,0:T(2,128)(2,1)}, u32[]{:S(2)}, u32[]{:S(2)}) %all-to-all-start.3) | async-done | bytes 1310752 | tf_op jit(solution)/shard_map/all_to_all | solution.py:106
  182.0 7.7 %reshape.118 = bf16[5120,1,1,128]{3,2,1,0:T(2,128)(2,1)S(1)} reshape(bf16[32,2,10240]{2,1,0:T(2,128)(2,1)} %all-to-all-done.3) | data formatting | bytes 2621440
  191.2 1.8 fusion.55
  193.7 2.0 collective-permute-start
  200.6 2.1 select_convert_fusion
  206.7 12.8 %fusion.46 = f32[4,6,8,6,384]{4,2,3,1,0:T(8,128)S(1)} fusion(bf16[3,3,3,384,384]{4,3,2,1,0:T(8,128)(2,1)S(1)} %bitcast.157, bf16[6,8,1,7,2,384]{5,3,4,1,0,2:T(8,128)(2,1)S(1)} %slice.11, bf16[6,8,1,8,6,384]{5,3,4,1,0,2:T(8,128)(2,1)S(1)} %copy.71, pred[8,6]{0,1:T(8,128)(4,1)S(1)} %copy-done.6), kind=kOutput, calls=%fused_computation.34 | convolution fusion | flops 9180463104 | bytes 12017712 | tf_op jit(solution)/shard_map/conv_general_dilated | solution.py:35
  (59 shorter events, 19.9 us)
Async XLA Ops:
  0.0 191.2 %copy-start = (bf16[4096,64]{0,1:T(8,128)(2,1)S(1)}, bf16[4096,64]{0,1:T(8,128)(2,1)}, u32[]{:S(2)}) copy-start(bf16[4096,64]{0,1:T(8,128)(2,1)} %param.16) | copy-start | bytes 1572868
  3.2 8.4 %copy-start.1 = (bf16[160,4096]{1,0:T(8,128)(2,1)S(1)}, bf16[160,4096]{1,0:T(8,128)(2,1)}, u32[]{:S(2)}) copy-start(bf16[160,4096]{1,0:T(8,128)(2,1)} %param.12) | copy-start | bytes 3932164
  3.2 28.3 %all-to-all-start = ((bf16[160,32,1,128]{3,0,2,1:T(8,128)(2,1)}), bf16[160,32,1,128]{3,0,2,1:T(8,128)(2,1)S(1)}, u32[]{:S(2)}, u32[]{:S(2)}) async-start(bf16[160,32,1,128]{3,0,2,1:T(8,128)(2,1)} %copy.58), calls=%async_computation | async-start | bytes 2621440 | tf_op jit(solution)/shard_map/all_to_all | solution.py:101
  31.6 23.9 %all-to-all-start.1 = ((bf16[160,32,1,128]{3,0,2,1:T(8,128)(2,1)}), bf16[160,32,1,128]{3,0,2,1:T(8,128)(2,1)S(1)}, u32[]{:S(2)}, u32[]{:S(2)}) async-start(bf16[160,32,1,128]{3,0,2,1:T(8,128)(2,1)} %copy.59), calls=%async_computation.1 | async-start | bytes 2621440 | tf_op jit(solution)/shard_map/all_to_all | solution.py:102
  55.5 24.6 %all-to-all-start.2 = ((bf16[160,32,1,128]{3,0,2,1:T(8,128)(2,1)}), bf16[160,32,1,128]{3,0,2,1:T(8,128)(2,1)}, u32[]{:S(2)}, u32[]{:S(2)}) async-start(bf16[160,32,1,128]{3,0,2,1:T(8,128)(2,1)} %copy.60), calls=%async_computation.2 | async-start | bytes 2621440 | tf_op jit(solution)/shard_map/all_to_all | solution.py:103
  157.2 5.0 %copy-start.4 = (s32[32]{0:T(128)S(1)}, s32[32]{0:T(128)}, u32[]{:S(2)}) copy-start(s32[32]{0:T(128)} %param.15) | copy-start | bytes 388
  157.2 24.7 %all-to-all-start.3 = ((bf16[32,2,10240]{2,1,0:T(2,128)(2,1)}), bf16[32,2,10240]{2,1,0:T(2,128)(2,1)}, u32[]{:S(2)}, u32[]{:S(2)}) async-start(bf16[32,2,10240]{2,1,0:T(2,128)(2,1)} %reshape.117), calls=%async_computation.3 | async-start | bytes 2621440 | tf_op jit(solution)/shard_map/all_to_all | solution.py:106
  191.2 2.5 %copy-start.2 = (bf16[4,4,640]{2,1,0:T(4,128)(2,1)S(1)}, bf16[4,4,640]{2,1,0:T(4,128)(2,1)}, u32[]{:S(2)}) copy-start(bf16[4,4,640]{2,1,0:T(4,128)(2,1)} %param.14) | copy-start | bytes 61444
  193.7 4.7 %collective-permute-start = (bf16[4,4,640]{2,1,0:T(4,128)(2,1)S(1)}, bf16[4,4,640]{2,1,0:T(4,128)(2,1)S(1)}, u32[]{:S(2)}, u32[]{:S(2)}) collective-permute-start(bf16[4,4,640]{2,1,0:T(4,128)(2,1)S(1)} %subtract_convert_fusion), channel_id=1, source_target_pairs={{0,1},{1,2},{2,3},{3,4},{4,5},{5,6},{6,7},{7,8},{8,9},{9,10},{10,1... | collective-permute-start | bytes 61448 | tf_op jit(solution)/shard_map/ppermute | solution.py:24
  195.8 3.1 %collective-permute-start.1 = (bf16[4,4,640]{2,1,0:T(4,128)(2,1)S(1)}, bf16[4,4,640]{2,1,0:T(4,128)(2,1)S(1)}, u32[]{:S(2)}, u32[]{:S(2)}) collective-permute-start(bf16[4,4,640]{2,1,0:T(4,128)(2,1)S(1)} %subtract_convert_fusion), channel_id=1, source_target_pairs={{1,0},{2,1},{3,2},{4,3},{5,4},{6,5},{7,6},{8,7},{9,8},{10,9},{11,1... | collective-permute-start | bytes 61448 | tf_op jit(solution)/shard_map/ppermute | solution.py:26
  199.7 1.0 copy-start.5
  199.7 1.0 copy-start.6
  203.0 0.7 copy-start.3
  203.0 2.3 %slice-start = ((s8[7962624]{0:T(1024)(128)(4,1)}), s8[4194304]{0:T(1024)(128)(4,1)S(1)}, s32[]{:S(2)}) async-start(s8[7962624]{0:T(1024)(128)(4,1)} %bitcast.156), calls=%async_computation.4 | async-start | bytes 8388608
  204.4 2.3 %slice-start.1 = ((s8[7962624]{0:T(1024)(128)(4,1)}), s8[3768320]{0:T(1024)(128)(4,1)S(1)}, s32[]{:S(2)}) async-start(s8[7962624]{0:T(1024)(128)(4,1)} %bitcast.156), calls=%async_computation.5 | async-start | bytes 7536640
where the time goes:
time: 228 us; the launch traced here: 223 us
  waiting for transfers between devices  73.4 us (32%)
  matrix products  70.6 us (31%)
  local copies, waits for them, and re-layouts  26.7 us (12%)
  other arithmetic  25.6 us (11%)
  starting transfers between devices  25.3 us (11%)
    dot_general x10, matrix products, attend_block(): jnp.einsum('hqk,khd->qhd', weights.astype(jnp.bfloat16), value_heads, pre...  37.9 us
    all_to_all x1, waiting for transfers between devices, per_device(): lax.all_to_all(values_in, 'seq', split_axis=1, concat_axis=0, tiled=True)  19.9 us
    reduce_sum x10, other arithmetic, attend_block(): totals = jnp.sum(weights, axis=2)  18.5 us
    all_to_all x1, waiting for transfers between devices, per_device(): lax.all_to_all(attended, 'seq', split_axis=0, concat_axis=1, tiled=True)  18.3 us
    all_to_all x1, waiting for transfers between devices, per_device(): lax.all_to_all(queries, 'seq', split_axis=1, concat_axis=0, tiled=True)  18.1 us
    all_to_all x1, waiting for transfers between devices, per_device(): lax.all_to_all(keys_in, 'seq', split_axis=1, concat_axis=0, tiled=True)  16.7 us
    dot_general x10, matrix products, attend_block(): jnp.einsum('qhd,khd->hqk', q_block, key_heads, preferred_element_type=jnp...  16 us
    conv_general_dilated x2, matrix products, causal_conv(): lax.conv_general_dilated(padded[None], weight, (1, 1, 1), 'VALID', dimens...  14.9 us
  transfers between devices with their start and end apart: 6, of which 5 were waited for; matrix products, arithmetic and copies ran while one was open for 3% of the time, Pallas kernels for 0%

commit v1 on v0

v1 whole, which is shorter than its diff:
```python
import functools
import math

import jax
import jax.numpy as jnp
from jax import lax
from jax.experimental import pallas as pl
from jax.experimental.pallas import tpu as pltpu
from jax.sharding import PartitionSpec as P

HEADS = 32
HEAD = 128
LAT_CH = 16
FRAMES = 4
BAND = 2
PCOLS = 20
TOK = 160
TOKENS = 5120
SEQ = 32
QB = 640
KB = 1280
NQ = TOKENS // QB
NK = TOKENS // KB
SCALE = math.log2(math.e) / math.sqrt(HEAD)
NEG = -1e30

CHIPS = (
    (0, 0), (1, 0), (3, 0), (0, 1), (0, 3), (1, 1), (3, 3), (1, 3),
    (3, 1), (2, 0), (0, 2), (2, 1), (1, 2), (2, 3), (3, 2), (2, 2),
)
ARRIVE = ("K0", "Q0", "Q1", "Q2", "Q3", "K1", "Q4", "Q5", "K2", "K3", "Q6", "Q7")


def plan_tiles():
    keys, queries, tiles = [], [], []
    for name in ARRIVE:
        place = int(name[1])
        if name[0] == "K":
            fresh = [(q, place) for q in queries]
            keys.append(place)
        else:
            fresh = [(place, k) for k in keys]
            queries.append(place)
        tiles += fresh
    seen_q, seen_k, rows = set(), set(), []
    for t, (q, k) in enumerate(tiles):
        last = all(u[0] != q for u in tiles[t + 1:])
        rows.append((q, k, int(q not in seen_q), int(k not in seen_k), int(last)))
        seen_q.add(q)
        seen_k.add(k)
    return rows


TILES = plan_tiles()


def packed_table(values, bits):
    per = 24 // bits
    words = []
    for at in range(0, len(values), per):
        word = 0
        for i, value in enumerate(values[at:at + per]):
            word |= value << (bits * i)
        words.append(word)

    def look(index):
        word = jnp.int32(words[0])
        for i in range(1, len(words)):
            word = jnp.where(index >= i * per, jnp.int32(words[i]), word)
        shift = lax.rem(index, per) * bits
        return lax.shift_right_logical(word, shift) & ((1 << bits) - 1)

    return look


def attend_kernel(
    q_hbm, k_hbm, v_hbm, w_ref, out_ref,
    v_in, v_send, q_got, k_got, v_got, q2, k2, v2, acc_ref, top_ref, s_ref, tile_top,
    y_send, y_got, in_sem, q_ssem, k_ssem, v_ssem, q_rsem, k_rsem, v_rsem, y_ssem, y_rsem,
):
    me = lax.axis_index("seq")
    my_x, my_z, my_c = me // 8, lax.rem(me // 2, 4), lax.rem(me, 2)
    look_dx = packed_table([c[0] for c in CHIPS], 2)
    look_dz = packed_table([c[1] for c in CHIPS], 2)

    def ahead(j):
        chip = j // 2
        x = lax.rem(my_x + look_dx(chip), 4)
        z = lax.rem(my_z + look_dz(chip), 4)
        return x * 8 + z * 2 + lax.rem(my_c + j, 2)

    def behind(j):
        chip = j // 2
        x = lax.rem(my_x + 4 - look_dx(chip), 4)
        z = lax.rem(my_z + 4 - look_dz(chip), 4)
        return x * 8 + z * 2 + lax.rem(my_c + j, 2)

    def head_cols(h):
        return pl.ds(pl.multiple_of(h * HEAD, HEAD), HEAD)

    def slot_rows(j):
        return pl.ds(pl.multiple_of(j * TOK, 32), TOK)

    def q_copy(j):
        to = ahead(j)
        return pltpu.make_async_remote_copy(
            src_ref=q_hbm.at[:, head_cols(to)], dst_ref=q_got.at[slot_rows(j)],
            send_sem=q_ssem.at[j], recv_sem=q_rsem.at[j],
            device_id={"seq": to}, device_id_type=pl.DeviceIdType.MESH,
        )

    def k_copy(j):
        to = ahead(j)
        return pltpu.make_async_remote_copy(
            src_ref=k_hbm.at[:, head_cols(to)], dst_ref=k_got.at[slot_rows(j)],
            send_sem=k_ssem.at[j], recv_sem=k_rsem.at[j],
            device_id={"seq": to}, device_id_type=pl.DeviceIdType.MESH,
        )

    def v_copy(j):
        return pltpu.make_async_remote_copy(
            src_ref=v_send.at[j], dst_ref=v_got.at[j],
            send_sem=v_ssem.at[j], recv_sem=v_rsem.at[j],
            device_id={"seq": ahead(j)}, device_id_type=pl.DeviceIdType.MESH,
        )

    def y_copy(j):
        return pltpu.make_async_remote_copy(
            src_ref=y_send.at[j], dst_ref=y_got.at[j],
            send_sem=y_ssem.at[j], recv_sem=y_rsem.at[j],
            device_id={"seq": behind(j)}, device_id_type=pl.DeviceIdType.MESH,
        )

    v_load = pltpu.make_async_copy(v_hbm, v_in, in_sem.at[0])
    q_own = pltpu.make_async_copy(q_hbm.at[:, head_cols(me)], q_got.at[pl.ds(0, TOK)], in_sem.at[1])
    k_own = pltpu.make_async_copy(k_hbm.at[:, head_cols(me)], k_got.at[pl.ds(0, TOK)], in_sem.at[2])
    v_load.start()
    q_own.start()
    k_own.start()
    barrier = pltpu.get_barrier_semaphore()

    def greet(j, carry):
        pl.semaphore_signal(
            barrier, inc=1, device_id={"seq": ahead(j)}, device_id_type=pl.DeviceIdType.MESH
        )
        return carry

    lax.fori_loop(1, SEQ, greet, 0)
    v_load.wait()

    def project(j):
        h = ahead(j)
        values = v_in[:, head_cols(h)]
        y = jnp.dot(values, w_ref[head_cols(h), :], preferred_element_type=jnp.float32)
        return jnp.concatenate([y[:80], y[80:]], axis=1).astype(jnp.bfloat16)

    def project_step(j, carry):
        v_send[j] = project(j)
        return carry

    lax.fori_loop(0, SEQ, project_step, 0, unroll=4)
    pl.semaphore_wait(barrier, SEQ - 1)

    def send_k(j, carry):
        k_copy(j).start()
        v_copy(j).start()
        return carry

    def send_q(j, carry):
        q_copy(j).start()
        return carry

    for name in ARRIVE:
        place = int(name[1])
        if name[0] == "K":
            lax.fori_loop(max(1, place * 8), place * 8 + 8, send_k, 0)
        else:
            lax.fori_loop(max(1, place * 4), place * 4 + 4, send_q, 0)

    def q_rows(i):
        return pl.ds(pl.multiple_of(i * QB, QB), QB)

    def k_rows(i):
        return pl.ds(pl.multiple_of(i * KB, KB), KB)

    def prep_q(i):
        def one(u, carry):
            j = i * 4 + u

            @pl.when(j == 0)
            def _():
                q_own.wait()

            @pl.when(j > 0)
            def _():
                q_copy(j).wait_recv()

            return carry

        lax.fori_loop(0, 4, one, 0)
        rows = q_rows(i)
        scaled = q_got[rows, :].astype(jnp.float32) * SCALE
        high = scaled.astype(jnp.bfloat16)
        q2[rows, :HEAD] = high
        q2[rows, HEAD:] = (scaled - high.astype(jnp.float32)).astype(jnp.bfloat16)
        acc_ref[rows, :] = jnp.zeros((QB, HEAD), jnp.float32)
        top_ref[rows, :] = jnp.full((QB, HEAD), NEG, jnp.float32)

    def prep_k(i):
        lane = lax.broadcasted_iota(jnp.int32, (80, HEAD), 1)
        ones = jnp.where(lane == 64, 1.0, 0.0)

        def one(u, carry):
            j = i * 8 + u

            @pl.when(j == 0)
            def _():
                k_own.wait()
                v_got[0] = v_send[0]

            @pl.when(j > 0)
            def _():
                k_copy(j).wait_recv()
                v_copy(j).wait_recv()

            both = v_got[j].astype(jnp.float32)
            left = jnp.where(lane < 64, both, ones)
            right = jnp.where(lane < 64, pltpu.roll(both, 64, 1), ones)
            at = pl.multiple_of(j * TOK, 32)
            v2[pl.ds(at, 80), :] = left.astype(jnp.bfloat16)
            v2[pl.ds(at + 80, 80), :] = right.astype(jnp.bfloat16)
            return carry

        lax.fori_loop(0, 8, one, 0)
        rows = k_rows(i)
        k2[rows, :HEAD] = k_got[rows, :]
        k2[rows, HEAD:] = k_got[rows, :]

    def finish(i):
        rows = q_rows(i)
        total = acc_ref[rows, :]
        y = total * (1.0 / total[:, 64:65])
        for u in range(4):
            j = i * 4 + u
            part = y[u * TOK:(u + 1) * TOK]
            merged = jnp.where(
                lax.broadcasted_iota(jnp.int32, (80, HEAD), 1) < 64,
                part[:80], pltpu.roll(part[80:], 64, 1),
            )
            y_send[j] = merged.astype(jnp.bfloat16)

        def one(u, carry):
            j = i * 4 + u

            @pl.when(j > 0)
            def _():
                y_copy(j).start()

            return carry

        lax.fori_loop(0, 4, one, 0)

    look_q = packed_table([t[0] for t in TILES], 3)
    look_k = packed_table([t[1] for t in TILES], 2)
    look_new_q = packed_table([t[2] for t in TILES], 1)
    look_new_k = packed_table([t[3] for t in TILES], 1)
    look_last = packed_table([t[4] for t in TILES], 1)

    def ready(t):
        @pl.when(look_new_k(t) == 1)
        def _():
            prep_k(look_k(t))

        @pl.when(look_new_q(t) == 1)
        def _():
            prep_q(look_q(t))

    def score(t, slot):
        s = lax.dot_general(
            q2[q_rows(look_q(t)), :], k2[k_rows(look_k(t)), :],
            (((1,), (1,)), ((), ())), preferred_element_type=jnp.float32,
        )
        s_ref[slot] = s
        top = s[:, :HEAD]
        for u in range(1, KB // HEAD):
            top = jnp.maximum(top, s[:, u * HEAD:(u + 1) * HEAD])
        tile_top[slot] = top

    def weigh(t, slot):
        rows = q_rows(look_q(t))
        before = top_ref[rows, :]
        now = jnp.maximum(before, jnp.max(tile_top[slot], axis=1, keepdims=True))
        top_ref[rows, :] = now
        weights = jnp.exp2(s_ref[slot] - jnp.concatenate([now] * (KB // HEAD), axis=1))
        acc_ref[rows, :] = acc_ref[rows, :] * jnp.exp2(before - now) + jnp.dot(
            weights.astype(jnp.bfloat16), v2[k_rows(look_k(t)), :],
            preferred_element_type=jnp.float32,
        )

    def after(t):
        @pl.when(look_last(t) == 1)
        def _():
            finish(look_q(t))

    def step(t, slot):
        ready(t + 1)
        score(t + 1, 1 - slot)
        weigh(t, slot)
        after(t)

    def two_steps(i, carry):
        step(2 * i, 0)
        step(2 * i + 1, 1)
        return carry

    count = len(TILES)
    ready(jnp.int32(0))
    score(jnp.int32(0), 0)
    lax.fori_loop(0, (count - 2) // 2, two_steps, 0)
    step(jnp.int32(count - 2), 0)
    weigh(jnp.int32(count - 1), 1)
    after(jnp.int32(count - 1))

    def gather(j, total):
        y_copy(j).wait_recv()
        return total + y_got[j].astype(jnp.float32)

    out_ref[...] = lax.fori_loop(1, SEQ, gather, y_send[0].astype(jnp.float32))

    def drain(j, carry):
        q_copy(j).wait_send()
        k_copy(j).wait_send()
        v_copy(j).wait_send()
        y_copy(j).wait_send()
        return carry

    lax.fori_loop(1, SEQ, drain, 0)


def attend(query, key, value, head_weight):
    bf16, f32 = jnp.bfloat16, jnp.float32
    any_space = pl.BlockSpec(memory_space=pl.ANY)
    vmem = pl.BlockSpec(memory_space=pltpu.VMEM)
    return pl.pallas_call(
        attend_kernel,
        out_shape=jax.ShapeDtypeStruct((80, HEAD), f32),
        in_specs=[any_space, any_space, any_space, vmem],
        out_specs=vmem,
        scratch_shapes=[
            pltpu.VMEM((TOK, HEADS * HEAD), bf16),
            pltpu.VMEM((SEQ, 80, HEAD), bf16),
            pltpu.VMEM((TOKENS, HEAD), bf16),
            pltpu.VMEM((TOKENS, HEAD), bf16),
            pltpu.VMEM((SEQ, 80, HEAD), bf16),
            pltpu.VMEM((TOKENS, 2 * HEAD), bf16),
            pltpu.VMEM((TOKENS, 2 * HEAD), bf16),
            pltpu.VMEM((TOKENS, HEAD), bf16),
            pltpu.VMEM((TOKENS, HEAD), f32),
            pltpu.VMEM((TOKENS, HEAD), f32),
            pltpu.VMEM((2, QB, KB), f32),
            pltpu.VMEM((2, QB, HEAD), f32),
            pltpu.VMEM((SEQ, 80, HEAD), bf16),
            pltpu.VMEM((SEQ, 80, HEAD), bf16),
            pltpu.SemaphoreType.DMA((3,)),
        ] + [pltpu.SemaphoreType.DMA((SEQ,))] * 8,
        compiler_params=pltpu.CompilerParams(
            collective_id=1, has_side_effects=True, vmem_limit_bytes=56 * 2**20
        ),
        cost_estimate=pl.CostEstimate(
            flops=4 * TOKENS * TOKENS * HEAD, bytes_accessed=16 * 2**20,
            transcendentals=TOKENS * TOKENS,
        ),
        name="attend",
    )(query, key, value, head_weight)


def with_halo(cells, width):
    count = lax.axis_size("seq")
    ends = count - 1
    head = cells[:, :width]
    tail = cells[:, cells.shape[1] - width:]
    return jnp.concatenate(
        [
            lax.ppermute(tail, "seq", [(i, i + 1) for i in range(ends)]),
            cells,
            lax.ppermute(head, "seq", [(i + 1, i) for i in range(ends)]),
        ],
        axis=1,
    )


def causal_conv(field, weight):
    padded = jnp.pad(field, ((2, 0), (0, 0), (1, 1), (0, 0)))
    return lax.conv_general_dilated(
        padded[None],
        weight,
        (1, 1, 1),
        "VALID",
        dimension_numbers=("NDHWC", "DHWIO", "NDHWC"),
        preferred_element_type=jnp.float32,
    )[0]


def decode_rows(window, first_row, total_rows, conv_in, conv_mid, gamma):
    first_conv = causal_conv(window, conv_in).astype(jnp.bfloat16)
    values32 = first_conv.astype(jnp.float32)
    row_ids = first_row + 1 + jnp.arange(first_conv.shape[1], dtype=jnp.int32)
    inside = (row_ids >= 0) & (row_ids < total_rows)
    normed = (
        values32 * lax.rsqrt(jnp.mean(values32 * values32, axis=-1, keepdims=True) + 1e-06) * gamma
    )
    normed = jnp.where(inside[None, :, None, None], jax.nn.silu(normed), 0.0).astype(jnp.bfloat16)
    mid_conv = causal_conv(normed, conv_mid)
    return (values32[:, 1:-1] + mid_conv).astype(jnp.bfloat16)


def per_device(query, key, value, latent, band_rows, head_weight, conv_in, conv_mid, gamma):
    place = lax.axis_index("seq")
    groups = lax.axis_size("seq")
    packed = attend(query, key, value, head_weight)
    velocity = jnp.concatenate([packed[:, :64], packed[:, 64:]], axis=0)
    band_len = 2 * BAND
    lat_cols = latent.shape[2] // LAT_CH
    grid = velocity.reshape(FRAMES, BAND, PCOLS, 2, 2, LAT_CH).transpose(0, 1, 3, 2, 4, 5)
    grid = grid.reshape(FRAMES, band_len, lat_cols * LAT_CH)
    clean = (latent.astype(jnp.float32) - 0.9 * grid).astype(jnp.bfloat16)
    window = with_halo(clean, 2)
    decoded = decode_rows(
        window.reshape(FRAMES, band_len + 4, lat_cols, LAT_CH),
        place * band_len - 2,
        band_len * groups,
        conv_in,
        conv_mid,
        gamma,
    )
    length = jnp.sum(jnp.where(jnp.arange(groups, dtype=jnp.int32) == place, band_rows, 0))
    extra = lax.ppermute(decoded[:, :BAND], "seq", [(i + 1, i) for i in range(0, groups, 2)])
    lead = jnp.where(lax.rem(place, 2) == 1, band_len - length, 0)
    extended = jnp.concatenate([decoded, extra, jnp.zeros_like(extra)], axis=1)
    picked = lax.dynamic_slice_in_dim(extended, lead, 3 * BAND, 1)
    keep_mask = jnp.arange(3 * BAND, dtype=jnp.int32) < length
    return jnp.where(keep_mask[None, :, None, None], picked, jnp.zeros_like(picked))


def solution(mesh):
    return jax.shard_map(
        per_device,
        mesh=mesh,
        in_specs=(
            P(("rep", "seq"), None),
            P(("rep", "seq"), None),
            P(("rep", "seq"), None),
            P("rep", "seq", None),
            P("rep"),
            P(),
            P(),
            P(),
            P(),
        ),
        out_specs=P("rep", "seq", None, None),
        check_vma=False,
    )
```

time: 228 us -> 118 us (0.52)
  the two profiles are of different devices: /device:TPU:0 before, /device:TPU:49 now
where the time goes in v1:
time: 118 us
  Pallas kernels  77.9 us (66%)
  starting transfers between devices  11.8 us (10%)
  matrix products  10.4 us (9%)
  local copies, waits for them, and re-layouts  9.15 us (8%)
  other arithmetic  4.82 us (4%)
  waiting for transfers between devices  2.86 us (2%)
    pallas_call x1, Pallas kernels, attend(): pl.pallas_call(attend_kernel, out_shape=jax.ShapeDtypeStruct((80, HEAD),...  77.9 us
    conv_general_dilated x2, matrix products, causal_conv(): lax.conv_general_dilated(padded[None], weight, (1, 1, 1), 'VALID', dimens...  10.4 us
    ppermute x1, starting transfers between devices, with_halo(): lax.ppermute(tail, 'seq', [(i, i + 1) for i in range(ends)])  8.37 us
    unnamed x16, local copies, waits for them, and re-layouts  2.88 us
    ppermute x1, waiting for transfers between devices, with_halo(): lax.ppermute(head, 'seq', [(i + 1, i) for i in range(ends)])  2.85 us
  transfers between devices with their start and end apart: 3, of which 1 were waited for; matrix products, arithmetic and copies ran while one was open for 1% of the time, Pallas kernels for 0%

profile of v1, /device:TPU:49, one launch (start us, length us, event | category | flops | bytes accessed | tf_op | source)
XLA Modules:
  0.0 117.9 jit_solution(9080757797687385745)
XLA Ops:
  0.0 0.0 copy-start
  0.0 2.4 %copy.25.w_ref = bf16[4096,64]{1,0:T(8,128)(2,1)} copy(bf16[4096,64]{0,1:T(8,128)(2,1)} %param.14) | data formatting | bytes 1048576 | tf_op args[5]
  2.4 77.9 %attend.1 = f32[80,128]{1,0:T(8,128)} custom-call(bf16[160,4096]{1,0:T(8,128)(2,1)} %q_hbm.1, bf16[160,4096]{1,0:T(8,128)(2,1)} %k_hbm.1, bf16[160,4096]{1,0:T(8,128)(2,1)} %v_hbm.1, bf16[4096,64]{1,0:T(8,128)(2,1)} %copy.25.w_ref), custom_call_target="tpu_custom_call" | custom-call | flops 13421772800 | bytes 16777216 | tf_op jit(solution)/shard_map/attend/pallas_call | solution.py:344
  80.3 0.0 copy-start.1
  80.3 0.9 fusion.31
  81.3 0.1 copy.27
  81.4 0.4 mul.43
  81.8 0.3 copy.28
  82.1 0.4 mul.45
  82.5 0.0 copy-done.1
  82.6 8.4 %collective-permute-start = (bf16[4,2,640]{2,1,0:T(2,128)(2,1)S(1)}, bf16[4,2,640]{2,1,0:T(2,128)(2,1)S(1)}, u32[]{:S(2)}, u32[]{:S(2)}) collective-permute-start(bf16[4,2,640]{2,1,0:T(2,128)(2,1)S(1)} %get-tuple-element.7), channel_id=1, source_target_pairs={{0,1},{1,2},{2,3},{3,4},{4,5},{5,6},{6,7},{7,8},{8,9},{9,10},{10,1... | collective-permute-start | bytes 30728 | tf_op jit(solution)/shard_map/ppermute | solution.py:384
  90.9 2.1 %collective-permute-start.1 = (bf16[4,2,640]{2,1,0:T(2,128)(2,1)S(1)}, bf16[4,2,640]{2,1,0:T(2,128)(2,1)S(1)}, u32[]{:S(2)}, u32[]{:S(2)}) collective-permute-start(bf16[4,2,640]{2,1,0:T(2,128)(2,1)S(1)} %get-tuple-element.8), channel_id=1, source_target_pairs={{1,0},{2,1},{3,2},{4,3},{5,4},{6,5},{7,6},{8,7},{9,8},{10,9},{11,1... | collective-permute-start | bytes 30728 | tf_op jit(solution)/shard_map/ppermute | solution.py:386
  93.1 0.0 collective-permute-done
  93.1 2.9 %collective-permute-done.1 = bf16[4,2,640]{2,1,0:T(2,128)(2,1)S(1)} collective-permute-done((bf16[4,2,640]{2,1,0:T(2,128)(2,1)S(1)}, bf16[4,2,640]{2,1,0:T(2,128)(2,1)S(1)}, u32[]{:S(2)}, u32[]{:S(2)}) %collective-permute-start.1) | collective-permute-done | bytes 10272 | tf_op jit(solution)/shard_map/ppermute | solution.py:386
  96.0 0.3 reshape.32
  96.3 0.1 pad_bitcast_fusion.1
  96.4 0.1 copy.42
  96.5 0.0 copy-start.4
  96.6 0.1 pad.10.clone
  96.7 0.0 slice-start
  96.7 0.2 copy.31
  96.9 0.1 slice.30
  96.9 0.0 copy-done
  96.9 0.3 copy-done.4
  97.2 1.9 %select_convert_fusion = bf16[4,6,8,6,384]{4,2,3,1,0:T(8,128)(2,1)S(1)} fusion(bf16[3,3,3,16,384]{4,3,2,1,0:T(8,128)(2,1)S(1)} %copy-done, pred[8,6]{0,1:T(8,128)(4,1)S(1)} %copy-done.4, bf16[6,8,1,7,2,16]{5,3,4,1,0,2:T(8,128)(2,1)S(1)} %slice.30, bf16[6,8,1,8,6,16]{5,3,4,1,0,2:T(8,128)(2,1)S(1)} %copy.31), kind=kOutput, calls=%fused_computation.8 | convolution fusion | flops 383385600 | bytes 1311792 | tf_op jit(solution)/shard_map/conv_general_dilated | solution.py:394
  99.2 0.5 copy.32
  99.6 0.0 copy-start.2
  99.6 0.5 multiply_reduce_fusion
  100.1 0.2 fusion.22
  100.3 1.2 select_convert_fusion.1
  101.5 0.5 pad_bitcast_fusion
  102.0 0.3 pad.12
  102.3 0.3 copy.35
  102.6 0.1 slice.33
  102.7 8.5 %fusion.9 = f32[4,4,8,6,384]{4,2,3,1,0:T(8,128)S(1)} fusion(bf16[3,3,3,384,384]{4,3,2,1,0:T(8,128)(2,1)S(1)} %bitcast.42, bf16[6,6,1,7,2,384]{5,3,4,1,0,2:T(8,128)(2,1)S(1)} %slice.33, bf16[6,6,1,8,6,384]{5,3,4,1,0,2:T(8,128)(2,1)S(1)} %copy.35, pred[8,6]{0,1:T(8,128)(4,1)S(1)} %copy-done.4), kind=kOutput, calls=%fused_computation.15 | convolution fusion | flops 6120898560 | bytes 10856496 | tf_op jit(solution)/shard_map/conv_general_dilated | solution.py:394
  111.2 0.5 copy.36
  111.6 0.2 slice.34
  111.8 0.0 copy-start.3
  111.8 0.7 fusion.12
  112.6 0.1 slice.35
  112.7 1.3 %collective-permute-start.2 = (bf16[4,2,40,384]{3,0,2,1:T(4,128)(2,1)S(1)}, bf16[4,2,40,384]{3,0,2,1:T(4,128)(2,1)S(1)}, u32[]{:S(2)}, u32[]{:S(2)}) collective-permute-start(bf16[4,2,40,384]{3,0,2,1:T(4,128)(2,1)S(1)} %slice.35), channel_id=1, source_target_pairs={{1,0},{3,2},{5,4},{7,6},{9,8},{11,10},{13,12},{15,14},{17,16},{19,... | collective-permute-start | bytes 737288 | tf_op jit(solution)/shard_map/ppermute | solution.py:437
  114.0 0.0 copy-done.3
  114.0 0.6 fusion.24
  115.3 0.7 iota_compare_fusion.2
  115.9 0.1 pad_dynamic-slice_fusion.2
  116.0 0.0 collective-permute-done.2
  116.0 0.9 broadcast_select_fusion
  116.9 1.0 copy.38
  (12 shorter events, 0.1 us)
Async XLA Ops:
  0.0 96.9 %copy-start = (bf16[3,3,3,16,384]{4,3,2,1,0:T(8,128)(2,1)S(1)}, bf16[3,3,3,16,384]{4,3,2,1,0:T(8,128)(2,1)}, u32[]{:S(2)}) copy-start(bf16[3,3,3,16,384]{4,3,2,1,0:T(8,128)(2,1)} %param.15) | copy-start | bytes 995332
  80.3 2.2 %copy-start.1 = (bf16[4,4,640]{2,1,0:T(4,128)(2,1)S(1)}, bf16[4,4,640]{2,1,0:T(4,128)(2,1)}, u32[]{:S(2)}) copy-start(bf16[4,4,640]{2,1,0:T(4,128)(2,1)} %param.12) | copy-start | bytes 61444
  82.6 10.5 %collective-permute-start = (bf16[4,2,640]{2,1,0:T(2,128)(2,1)S(1)}, bf16[4,2,640]{2,1,0:T(2,128)(2,1)S(1)}, u32[]{:S(2)}, u32[]{:S(2)}) collective-permute-start(bf16[4,2,640]{2,1,0:T(2,128)(2,1)S(1)} %get-tuple-element.7), channel_id=1, source_target_pairs={{0,1},{1,2},{2,3},{3,4},{4,5},{5,6},{6,7},{7,8},{8,9},{9,10},{10,1... | collective-permute-start | bytes 30728 | tf_op jit(solution)/shard_map/ppermute | solution.py:384
  90.9 5.0 %collective-permute-start.1 = (bf16[4,2,640]{2,1,0:T(2,128)(2,1)S(1)}, bf16[4,2,640]{2,1,0:T(2,128)(2,1)S(1)}, u32[]{:S(2)}, u32[]{:S(2)}) collective-permute-start(bf16[4,2,640]{2,1,0:T(2,128)(2,1)S(1)} %get-tuple-element.8), channel_id=1, source_target_pairs={{1,0},{2,1},{3,2},{4,3},{5,4},{6,5},{7,6},{8,7},{9,8},{10,9},{11,1... | collective-permute-start | bytes 30728 | tf_op jit(solution)/shard_map/ppermute | solution.py:386
  96.5 0.7 copy-start.4
  96.7 6.0 %slice-start = ((s8[7962624]{0:T(1024)(128)(4,1)}), s8[4194304]{0:T(1024)(128)(4,1)S(1)}, s32[]{:S(2)}) async-start(s8[7962624]{0:T(1024)(128)(4,1)} %bitcast.41), calls=%async_computation | async-start | bytes 8388608
  97.2 5.5 %slice-start.1 = ((s8[7962624]{0:T(1024)(128)(4,1)}), s8[3768320]{0:T(1024)(128)(4,1)S(1)}, s32[]{:S(2)}) async-start(s8[7962624]{0:T(1024)(128)(4,1)} %bitcast.41), calls=%async_computation.1 | async-start | bytes 7536640
  99.6 0.7 copy-start.2
  111.8 2.2 %copy-start.3 = (s32[32]{0:T(128)S(1)}, s32[32]{0:T(128)}, u32[]{:S(2)}) copy-start(s32[32]{0:T(128)} %param.13) | copy-start | bytes 388
  112.7 3.4 %collective-permute-start.2 = (bf16[4,2,40,384]{3,0,2,1:T(4,128)(2,1)S(1)}, bf16[4,2,40,384]{3,0,2,1:T(4,128)(2,1)S(1)}, u32[]{:S(2)}, u32[]{:S(2)}) collective-permute-start(bf16[4,2,40,384]{3,0,2,1:T(4,128)(2,1)S(1)} %slice.35), channel_id=1, source_target_pairs={{1,0},{3,2},{5,4},{7,6},{9,8},{11,10},{13,12},{15,14},{17,16},{19,... | collective-permute-start | bytes 737288 | tf_op jit(solution)/shard_map/ppermute | solution.py:437

commit v2 on v1

v2 whole, which is shorter than its diff:
```python
import functools
import math

import jax
import jax.numpy as jnp
from jax import lax
from jax.experimental import pallas as pl
from jax.experimental.pallas import tpu as pltpu
from jax.sharding import PartitionSpec as P

HEADS = 32
HEAD = 128
LAT_CH = 16
CH = 384
FRAMES = 4
BAND = 2
PCOLS = 20
LCOLS = 40
TOK = 160
TOKENS = 5120
SEQ = 32
QB = 640
KB = 1280
NQ = TOKENS // QB
NK = TOKENS // KB
SCALE = math.log2(math.e) / math.sqrt(HEAD)
NEG = -1e30
V_AFTER = 1

CHIPS = (
    (0, 0), (1, 0), (3, 0), (0, 1), (0, 3), (1, 1), (3, 3), (1, 3),
    (3, 1), (2, 0), (0, 2), (2, 1), (1, 2), (2, 3), (3, 2), (2, 2),
)
ARRIVE = ("K0", "Q0", "Q1", "Q2", "Q3", "K1", "Q4", "Q5", "K2", "K3", "Q6", "Q7")


def plan_tiles():
    keys, queries, tiles = [], [], []
    for name in ARRIVE:
        place = int(name[1])
        if name[0] == "K":
            fresh = [(q, place) for q in queries]
            keys.append(place)
        else:
            fresh = [(place, k) for k in keys]
            queries.append(place)
        tiles += fresh
    seen_q, seen_k, rows = set(), set(), []
    for t, (q, k) in enumerate(tiles):
        last = all(u[0] != q for u in tiles[t + 1:])
        rows.append((q, k, int(q not in seen_q), int(k not in seen_k), int(last)))
        seen_q.add(q)
        seen_k.add(k)
    return rows


TILES = plan_tiles()


def packed_table(values, bits):
    per = 24 // bits
    words = []
    for at in range(0, len(values), per):
        word = 0
        for i, value in enumerate(values[at:at + per]):
            word |= value << (bits * i)
        words.append(word)

    def look(index):
        word = jnp.int32(words[0])
        for i in range(1, len(words)):
            word = jnp.where(index >= i * per, jnp.int32(words[i]), word)
        shift = lax.rem(index, per) * bits
        return lax.shift_right_logical(word, shift) & ((1 << bits) - 1)

    return look


def attend_kernel(
    q_hbm, k_hbm, v_hbm, w_hbm, out_ref,
    v_in, w_in, v_send, q_got, k_got, v_got, q2, k2, v2, acc_ref, top_ref, s_ref, tile_top,
    y_send, y_got, in_sem, send_sem, q_sem, k_sem, v_sem, y_sem,
):
    me = lax.axis_index("seq")
    my_x, my_z, my_c = me // 8, lax.rem(me // 2, 4), lax.rem(me, 2)
    look_dx = packed_table([c[0] for c in CHIPS], 2)
    look_dz = packed_table([c[1] for c in CHIPS], 2)

    def ahead(j):
        chip = j // 2
        x = lax.rem(my_x + look_dx(chip), 4)
        z = lax.rem(my_z + look_dz(chip), 4)
        return x * 8 + z * 2 + lax.rem(my_c + j, 2)

    def behind(j):
        chip = j // 2
        x = lax.rem(my_x + 4 - look_dx(chip), 4)
        z = lax.rem(my_z + 4 - look_dz(chip), 4)
        return x * 8 + z * 2 + lax.rem(my_c + j, 2)

    def head_cols(h):
        return pl.ds(pl.multiple_of(h * HEAD, HEAD), HEAD)

    def slot_rows(j):
        return pl.ds(pl.multiple_of(j * TOK, 32), TOK)

    def push(source, target, to, which, sem):
        pltpu.make_async_remote_copy(
            src_ref=source, dst_ref=target, send_sem=send_sem.at[which], recv_sem=sem,
            device_id={"seq": to}, device_id_type=pl.DeviceIdType.MESH,
        ).start()

    def arrived(ref, sem):
        pltpu.make_async_copy(ref, ref, sem).wait()

    v_load = pltpu.make_async_copy(v_hbm, v_in, in_sem.at[0])
    w_load = pltpu.make_async_copy(w_hbm, w_in, in_sem.at[1])
    v_load.start()
    w_load.start()
    pltpu.make_async_copy(k_hbm.at[:, head_cols(me)], k_got.at[pl.ds(0, TOK)], k_sem.at[0]).start()
    pltpu.make_async_copy(q_hbm.at[:, head_cols(me)], q_got.at[pl.ds(0, TOK)], q_sem.at[0]).start()
    barrier = pltpu.get_barrier_semaphore()

    def greet(j, carry):
        pl.semaphore_signal(
            barrier, inc=1, device_id={"seq": ahead(j)}, device_id_type=pl.DeviceIdType.MESH
        )
        return carry

    lax.fori_loop(1, SEQ, greet, 0)
    pl.semaphore_wait(barrier, SEQ - 1)

    def send_k(j, carry):
        to = ahead(j)
        push(k_hbm.at[:, head_cols(to)], k_got.at[slot_rows(j)], to, 0, k_sem.at[j // 8])
        return carry

    def send_q(j, carry):
        to = ahead(j)
        push(q_hbm.at[:, head_cols(to)], q_got.at[slot_rows(j)], to, 1, q_sem.at[j // 4])
        return carry

    def send_v(j, carry):
        push(v_send.at[j], v_got.at[j], ahead(j), 2, v_sem.at[j // 8])
        return carry

    def project(j, carry):
        h = ahead(j)
        y = lax.dot_general(
            v_in[:, head_cols(h)], w_in[:, head_cols(h)],
            (((1,), (1,)), ((), ())), preferred_element_type=jnp.float32,
        )
        v_send[j] = jnp.concatenate([y[:80], y[80:]], axis=1).astype(jnp.bfloat16)
        return carry

    pending = []
    for at, name in enumerate(ARRIVE):
        place = int(name[1])
        if name[0] == "K":
            lax.fori_loop(max(1, place * 8), place * 8 + 8, send_k, 0)
            pending.append(place)
        else:
            lax.fori_loop(max(1, place * 4), place * 4 + 4, send_q, 0)
        if at >= V_AFTER and pending:
            if pending[0] == 0:
                v_load.wait()
                w_load.wait()
            for chunk in pending:
                lax.fori_loop(chunk * 8, chunk * 8 + 8, project, 0, unroll=4)
                lax.fori_loop(max(1, chunk * 8), chunk * 8 + 8, send_v, 0)
            if pending[0] == 0:
                pltpu.make_async_copy(v_send.at[0], v_got.at[0], v_sem.at[0]).start()
            pending = []

    def q_rows(i):
        return pl.ds(pl.multiple_of(i * QB, QB), QB)

    def k_rows(i):
        return pl.ds(pl.multiple_of(i * KB, KB), KB)

    def prep_q(i):
        rows = q_rows(i)
        arrived(q_got.at[rows], q_sem.at[i])
        scaled = q_got[rows, :].astype(jnp.float32) * SCALE
        high = scaled.astype(jnp.bfloat16)
        q2[rows, :HEAD] = high
        q2[rows, HEAD:] = (scaled - high.astype(jnp.float32)).astype(jnp.bfloat16)
        acc_ref[rows, :] = jnp.zeros((QB, HEAD), jnp.float32)
        top_ref[rows, :] = jnp.full((QB, HEAD), NEG, jnp.float32)

    def prep_k(i):
        lane = lax.broadcasted_iota(jnp.int32, (80, HEAD), 1)
        ones = jnp.where(lane == 64, 1.0, 0.0)
        rows = k_rows(i)
        arrived(k_got.at[rows], k_sem.at[i])
        k2[rows, :HEAD] = k_got[rows, :]
        k2[rows, HEAD:] = k_got[rows, :]
        slots = pl.ds(pl.multiple_of(i * 8, 8), 8)
        arrived(v_got.at[slots], v_sem.at[i])
        for u in range(8):
            j = i * 8 + u
            both = v_got[j].astype(jnp.float32)
            left = jnp.where(lane < 64, both, ones)
            right = jnp.where(lane < 64, pltpu.roll(both, 64, 1), ones)
            at = pl.multiple_of(j * TOK, 32)
            v2[pl.ds(at, 80), :] = left.astype(jnp.bfloat16)
            v2[pl.ds(at + 80, 80), :] = right.astype(jnp.bfloat16)

    def finish(i):
        rows = q_rows(i)
        total = acc_ref[rows, :]
        y = total * (1.0 / total[:, 64:65])
        for u in range(4):
            j = i * 4 + u
            part = y[u * TOK:(u + 1) * TOK]
            merged = jnp.where(
                lax.broadcasted_iota(jnp.int32, (80, HEAD), 1) < 64,
                part[:80], pltpu.roll(part[80:], 64, 1),
            )
            y_send[j] = merged.astype(jnp.bfloat16)

        def one(u, carry):
            j = i * 4 + u

            @pl.when(j > 0)
            def _():
                push(y_send.at[j], y_got.at[j], behind(j), 3, y_sem)

            return carry

        lax.fori_loop(0, 4, one, 0)

    look_q = packed_table([t[0] for t in TILES], 3)
    look_k = packed_table([t[1] for t in TILES], 2)
    look_new_q = packed_table([t[2] for t in TILES], 1)
    look_new_k = packed_table([t[3] for t in TILES], 1)
    look_last = packed_table([t[4] for t in TILES], 1)

    def ready(t):
        @pl.when(look_new_k(t) == 1)
        def _():
            prep_k(look_k(t))

        @pl.when(look_new_q(t) == 1)
        def _():
            prep_q(look_q(t))

    def score(t, slot):
        s = lax.dot_general(
            q2[q_rows(look_q(t)), :], k2[k_rows(look_k(t)), :],
            (((1,), (1,)), ((), ())), preferred_element_type=jnp.float32,
        )
        s_ref[slot] = s
        top = s[:, :HEAD]
        for u in range(1, KB // HEAD):
            top = jnp.maximum(top, s[:, u * HEAD:(u + 1) * HEAD])
        tile_top[slot] = top

    def weigh(t, slot):
        rows = q_rows(look_q(t))
        before = top_ref[rows, :]
        now = jnp.maximum(before, jnp.max(tile_top[slot], axis=1, keepdims=True))
        top_ref[rows, :] = now
        weights = jnp.exp2(s_ref[slot] - jnp.concatenate([now] * (KB // HEAD), axis=1))
        acc_ref[rows, :] = acc_ref[rows, :] * jnp.exp2(before - now) + jnp.dot(
            weights.astype(jnp.bfloat16), v2[k_rows(look_k(t)), :],
            preferred_element_type=jnp.float32,
        )

    def after(t):
        @pl.when(look_last(t) == 1)
        def _():
            finish(look_q(t))

    def step(t, slot):
        ready(t + 1)
        score(t + 1, 1 - slot)
        weigh(t, slot)
        after(t)

    def two_steps(i, carry):
        step(2 * i, 0)
        step(2 * i + 1, 1)
        return carry

    count = len(TILES)
    ready(jnp.int32(0))
    score(jnp.int32(0), 0)
    lax.fori_loop(0, (count - 2) // 2, two_steps, 0)
    step(jnp.int32(count - 2), 0)
    weigh(jnp.int32(count - 1), 1)
    after(jnp.int32(count - 1))

    others = pl.ds(1, SEQ - 1)
    arrived(y_got.at[others], y_sem)

    def gather(j, total):
        return total + y_got[j].astype(jnp.float32)

    out_ref[...] = lax.fori_loop(1, SEQ, gather, y_send[0].astype(jnp.float32), unroll=True)
    arrived(k_got.at[pl.ds(TOK, TOKENS - TOK)], send_sem.at[0])
    arrived(q_got.at[pl.ds(TOK, TOKENS - TOK)], send_sem.at[1])
    arrived(v_got.at[others], send_sem.at[2])
    arrived(y_got.at[others], send_sem.at[3])


def attend(query, key, value, head_weight):
    bf16, f32 = jnp.bfloat16, jnp.float32
    any_space = pl.BlockSpec(memory_space=pl.ANY)
    return pl.pallas_call(
        attend_kernel,
        out_shape=jax.ShapeDtypeStruct((80, HEAD), f32),
        in_specs=[any_space] * 4,
        out_specs=pl.BlockSpec(memory_space=pltpu.VMEM),
        scratch_shapes=[
            pltpu.VMEM((TOK, HEADS * HEAD), bf16),
            pltpu.VMEM((64, HEADS * HEAD), bf16),
            pltpu.VMEM((SEQ, 80, HEAD), bf16),
            pltpu.VMEM((TOKENS, HEAD), bf16),
            pltpu.VMEM((TOKENS, HEAD), bf16),
            pltpu.VMEM((SEQ, 80, HEAD), bf16),
            pltpu.VMEM((TOKENS, 2 * HEAD), bf16),
            pltpu.VMEM((TOKENS, 2 * HEAD), bf16),
            pltpu.VMEM((TOKENS, HEAD), bf16),
            pltpu.VMEM((TOKENS, HEAD), f32),
            pltpu.VMEM((TOKENS, HEAD), f32),
            pltpu.VMEM((2, QB, KB), f32),
            pltpu.VMEM((2, QB, HEAD), f32),
            pltpu.VMEM((SEQ, 80, HEAD), bf16),
            pltpu.VMEM((SEQ, 80, HEAD), bf16),
            pltpu.SemaphoreType.DMA((2,)),
            pltpu.SemaphoreType.DMA((4,)),
            pltpu.SemaphoreType.DMA((NQ,)),
            pltpu.SemaphoreType.DMA((NK,)),
            pltpu.SemaphoreType.DMA((NK,)),
            pltpu.SemaphoreType.DMA,
        ],
        compiler_params=pltpu.CompilerParams(
            collective_id=1, has_side_effects=True, vmem_limit_bytes=56 * 2**20
        ),
        cost_estimate=pl.CostEstimate(
            flops=4 * TOKENS * TOKENS * HEAD, bytes_accessed=16 * 2**20,
            transcendentals=TOKENS * TOKENS,
        ),
        name="attend",
    )(query, key, value, head_weight.T)


def decode_kernel(
    vel_ref, lat_ref, w_first, w_mid, gamma_ref, out_ref,
    turned, win, own, above, below, near, first_in, w1, first, wide, taps, total, w2, extra,
    in_sem, halo_ssem, halo_rsem, pair_sem,
):
    me = lax.axis_index("seq")
    up, down = lax.rem(me + SEQ - 1, SEQ), lax.rem(me + 1, SEQ)
    odd = lax.rem(me, 2)
    bf16, f32 = jnp.bfloat16, jnp.float32
    w_load = pltpu.make_async_copy(w_mid, w2, in_sem.at[0])
    w_load.start()
    barrier = pltpu.get_barrier_semaphore()
    for to in (up, down):
        pl.semaphore_signal(
            barrier, inc=1, device_id={"seq": to}, device_id_type=pl.DeviceIdType.MESH
        )

    lane20 = lax.broadcasted_iota(jnp.int32, (80, HEAD), 1)
    vel = vel_ref[...]
    for o in range(8):
        turn = vel if o == 0 else pltpu.roll(vel, HEAD - LAT_CH * o, 1)
        turned[o] = jnp.where(lane20 < LAT_CH, turn, 0.0)
    win[...] = jnp.zeros_like(win)
    for f in range(FRAMES):
        for r in range(BAND):
            for a in range(2):
                for b in range(2):
                    o = (f // 2) * 4 + a * 2 + b
                    row = f * 8 + 2 + 2 * r + a
                    win[row, pl.ds(8 + b, PCOLS, stride=2), :] = turned[
                        o, pl.ds(((f % 2) * BAND + r) * PCOLS, PCOLS), :
                    ]
    own[:, LCOLS:, :] = jnp.zeros((4, 8, HEAD), f32)
    for y in range(4):
        merged = jnp.zeros((LCOLS, HEAD), f32)
        for f in range(FRAMES):
            grid = win[f * 8 + 2 + y, 8:48, :]
            clean = (lat_ref[f * 4 + y] - 0.9 * grid).astype(bf16).astype(f32)
            win[f * 8 + 2 + y, 8:48, :] = clean
            merged = merged + (clean if f == 0 else pltpu.roll(clean, LAT_CH * f, 1))
        own[y, 0:LCOLS, :] = merged
    near[0] = own[0:2].astype(bf16)
    near[1] = own[2:4].astype(bf16)
    pl.semaphore_wait(barrier, 2)
    to_up = pltpu.make_async_remote_copy(
        src_ref=near.at[0], dst_ref=below, send_sem=halo_ssem.at[0], recv_sem=halo_rsem.at[0],
        device_id={"seq": up}, device_id_type=pl.DeviceIdType.MESH,
    )
    to_down = pltpu.make_async_remote_copy(
        src_ref=near.at[1], dst_ref=above, send_sem=halo_ssem.at[1], recv_sem=halo_rsem.at[1],
        device_id={"seq": down}, device_id_type=pl.DeviceIdType.MESH,
    )
    to_up.start()
    to_down.start()

    w1[...] = jnp.zeros_like(w1)
    for s in range(3):
        w1[s * HEAD:s * HEAD + 48, :] = w_first[s * 3]
        w1[s * HEAD + 64:s * HEAD + 112, :] = w_first[s * 3 + 1]
    w1[384:432, :] = w_first[2]
    w1[448:496, :] = w_first[5]
    w1[512:560, :] = w_first[8]
    wide[:, 0:8, :] = jnp.zeros((FRAMES * 6, 8, CH), f32)
    wide[:, 48:56, :] = jnp.zeros((FRAMES * 6, 8, CH), f32)

    to_up.wait_recv()
    to_down.wait_recv()
    lane40 = lax.broadcasted_iota(jnp.int32, (LCOLS, HEAD), 1)
    for side in range(2):
        there = (me > 0) if side == 0 else (me < SEQ - 1)
        got = above if side == 0 else below
        for y in range(2):
            rows = jnp.where(there, got[y, 0:LCOLS, :].astype(f32), 0.0)
            for f in range(FRAMES):
                part = rows if f == 0 else pltpu.roll(rows, HEAD - LAT_CH * f, 1)
                win[f * 8 + (0 if side == 0 else 6) + y, 8:48, :] = jnp.where(
                    lane40 < LAT_CH, part, 0.0
                )

    def gather_columns(f, carry):
        parts = []
        for y in range(8):
            row = f * 8 + y
            parts.append(
                win[row, 7:47, :]
                + pltpu.roll(win[row, 8:48, :], LAT_CH, 1)
                + pltpu.roll(win[row, 9:49, :], 2 * LAT_CH, 1)
            )
        block = jnp.concatenate(parts, axis=0)
        pair = block[0:240] + pltpu.roll(block[40:280], 64, 1)
        single = block[80:320]
        first_in[f, :, 256:384] = pair.astype(bf16)
        first_in[f, :, 512:640] = single.astype(bf16)
        for later in (1, 2):
            @pl.when(f + later < FRAMES)
            def _():
                first_in[f + later, :, (2 - later) * HEAD:(3 - later) * HEAD] = pair.astype(bf16)

        total[f] = single
        return carry

    lax.fori_loop(0, FRAMES, gather_columns, 0)
    blank = jnp.zeros((240, HEAD), bf16)
    first_in[0, :, 0:128] = blank
    first_in[0, :, 128:256] = blank
    first_in[1, :, 0:128] = blank
    first_in[0, :, 384:512] = blank
    first_in[1, :, 384:512] = pltpu.roll(total[0], 64, 1).astype(bf16)
    first_in[2, :, 384:512] = (total[0] + pltpu.roll(total[1], 64, 1)).astype(bf16)
    first_in[3, :, 384:512] = (total[1] + pltpu.roll(total[2], 64, 1)).astype(bf16)

    def first_step(f, carry):
        conv = jnp.dot(first_in[f], w1[...], preferred_element_type=f32)
        values = conv.astype(bf16).astype(f32)
        power = jnp.mean(values * values, axis=1, keepdims=True)
        normed = values * lax.rsqrt(power + 1e-06) * gamma_ref[...]
        normed = normed / (1.0 + jnp.exp(-normed))
        place = lax.broadcasted_iota(jnp.int32, (240, CH), 0)
        outside = ((place < 40) & (me == 0)) | ((place >= 200) & (me == SEQ - 1))
        normed = jnp.where(outside, 0.0, normed)
        first[f] = values[40:200]
        for y in range(6):
            wide[f * 6 + y, 8:48, :] = normed[y * 40:(y + 1) * 40]
        for u in range(3):
            for w in range(3):
                rows = [wide[f * 6 + y + u, 7 + w:47 + w, :] for y in range(4)]
                at = (u * 3 + w) * CH
                taps[f, :, at:at + CH] = jnp.concatenate(rows, axis=0).astype(bf16)
        return carry

    lax.fori_loop(0, FRAMES, first_step, 0)
    w_load.wait()
    for s in (2, 1, 0):
        count = FRAMES - (2 - s)
        for part in range(3):
            cols = slice(part * 3 * CH, (part + 1) * 3 * CH)
            term = jnp.dot(
                taps[0:count, :, cols].reshape(count * TOK, 3 * CH), w2[s, cols, :],
                preferred_element_type=f32,
            ).reshape(count, TOK, CH)
            first[2 - s:FRAMES] = first[2 - s:FRAMES] + term

    out_ref[:, 0:TOK, :] = first[...].astype(bf16)
    hand = pltpu.make_async_remote_copy(
        src_ref=out_ref.at[:, pl.ds(0, 80), :], dst_ref=extra,
        send_sem=pair_sem.at[0], recv_sem=pair_sem.at[1],
        device_id={"seq": me - odd}, device_id_type=pl.DeviceIdType.MESH,
    )

    @pl.when(odd == 1)
    def _():
        hand.start()
        hand.wait_send()
        out_ref[:, TOK:TOK + 80, :] = jnp.zeros((FRAMES, 80, CH), bf16)

    @pl.when(odd == 0)
    def _():
        hand.wait_recv()
        out_ref[:, TOK:TOK + 80, :] = extra[...]

    to_up.wait_send()
    to_down.wait_send()


def decode(velocity, latent, conv_in, conv_mid, gamma):
    bf16, f32 = jnp.bfloat16, jnp.float32
    vmem = pl.BlockSpec(memory_space=pltpu.VMEM)
    spaced = latent.reshape(FRAMES * 4, LCOLS, LAT_CH).astype(f32)
    spaced = jnp.pad(spaced, ((0, 0), (0, 0), (0, HEAD - LAT_CH)))
    return pl.pallas_call(
        decode_kernel,
        out_shape=jax.ShapeDtypeStruct((FRAMES, TOK + 80, CH), bf16),
        in_specs=[vmem, vmem, vmem, pl.BlockSpec(memory_space=pl.ANY), vmem],
        out_specs=vmem,
        scratch_shapes=[
            pltpu.VMEM((8, 80, HEAD), f32),
            pltpu.VMEM((FRAMES * 8, 56, HEAD), f32),
            pltpu.VMEM((4, 48, HEAD), f32),
            pltpu.VMEM((2, 48, HEAD), bf16),
            pltpu.VMEM((2, 48, HEAD), bf16),
            pltpu.VMEM((2, 2, 48, HEAD), bf16),
            pltpu.VMEM((FRAMES, 240, 640), bf16),
            pltpu.VMEM((640, CH), bf16),
            pltpu.VMEM((FRAMES, TOK, CH), f32),
            pltpu.VMEM((FRAMES * 6, 56, CH), f32),
            pltpu.VMEM((FRAMES, TOK, 9 * CH), bf16),
            pltpu.VMEM((FRAMES, 240, HEAD), f32),
            pltpu.VMEM((3, 9 * CH, CH), bf16),
            pltpu.VMEM((FRAMES, 80, CH), bf16),
            pltpu.SemaphoreType.DMA((1,)),
            pltpu.SemaphoreType.DMA((2,)),
            pltpu.SemaphoreType.DMA((2,)),
            pltpu.SemaphoreType.DMA((2,)),
        ],
        compiler_params=pltpu.CompilerParams(
            collective_id=2, has_side_effects=True, vmem_limit_bytes=48 * 2**20
        ),
        cost_estimate=pl.CostEstimate(
            flops=2 * 640 * 27 * CH * CH, bytes_accessed=10 * 2**20, transcendentals=960 * CH
        ),
        name="decode",
    )(
        velocity, spaced, conv_in.reshape(9, 48, CH), conv_mid.reshape(3, 9 * CH, CH),
        gamma.reshape(1, CH),
    )


def per_device(query, key, value, latent, band_rows, head_weight, conv_in, conv_mid, gamma):
    place = lax.axis_index("seq")
    velocity = attend(query, key, value, head_weight)
    decoded = decode(velocity, latent, conv_in, conv_mid, gamma)
    decoded = decoded.reshape(FRAMES, 3 * BAND, LCOLS, CH)
    groups = lax.axis_size("seq")
    length = jnp.sum(jnp.where(jnp.arange(groups, dtype=jnp.int32) == place, band_rows, 0))
    lead = jnp.where(lax.rem(place, 2) == 1, 2 * BAND - length, 0)
    extended = jnp.pad(decoded, ((0, 0), (0, BAND), (0, 0), (0, 0)))
    picked = lax.dynamic_slice_in_dim(extended, lead, 3 * BAND, 1)
    keep_mask = jnp.arange(3 * BAND, dtype=jnp.int32) < length
    return jnp.where(keep_mask[None, :, None, None], picked, jnp.zeros_like(picked))


def solution(mesh):
    return jax.shard_map(
        per_device,
        mesh=mesh,
        in_specs=(
            P(("rep", "seq"), None),
            P(("rep", "seq"), None),
            P(("rep", "seq"), None),
            P("rep", "seq", None),
            P("rep"),
            P(),
            P(),
            P(),
            P(),
        ),
        out_specs=P("rep", "seq", None, None),
        check_vma=False,
    )
```

time: 118 us -> 93.4 us (0.79)
  the two profiles are of different devices: /device:TPU:49 before, /device:TPU:0 now
where the time goes in v2:
time: 93.4 us; the launch traced here: 92.2 us
  Pallas kernels  86.8 us (93%)
  other arithmetic  3 us (3%)
  local copies, waits for them, and re-layouts  1.65 us (2%)
    pallas_call x1, Pallas kernels, attend(): pl.pallas_call(attend_kernel, out_shape=jax.ShapeDtypeStruct((80, HEAD),...  69.5 us
    pallas_call x1, Pallas kernels, decode(): pl.pallas_call(decode_kernel, out_shape=jax.ShapeDtypeStruct((FRAMES, TOK...  17.2 us

profile of v2, /device:TPU:0, one launch (start us, length us, event | category | flops | bytes accessed | tf_op | source)
XLA Modules:
  0.0 92.2 jit_solution(14130628940783347406)
XLA Ops:
  0.0 1.3 %fusion.1 = s32[]{:T(128)} fusion(s32[32]{0:T(128)} %param.13, s32[]{:T(128)S(6)} %axis_index.12), kind=kLoop, calls=%fused_computation.4 | loop fusion | flops 95 | bytes 136 | tf_op jit(solution)/shard_map/reduce_sum | solution.py:562
  2.0 0.7 iota_compare_fusion
  2.6 0.7 reshape.21.gamma_ref
  3.3 0.0 copy-start.2
  3.3 0.0 copy-start
  3.3 69.5 %attend.1.vel_ref = f32[80,128]{1,0:T(8,128)} custom-call(bf16[160,4096]{1,0:T(8,128)(2,1)} %q_hbm.1, bf16[160,4096]{1,0:T(8,128)(2,1)} %k_hbm.1, bf16[160,4096]{1,0:T(8,128)(2,1)} %v_hbm.1, bf16[64,4096]{1,0:T(8,128)(2,1)} %bitcast.7), custom_call_target="tpu_custom_call" | custom-call | flops 13421772800 | bytes 16777216 | tf_op jit(solution)/shard_map/attend/pallas_call | solution.py:310
  72.9 0.0 copy-done.2
  72.9 0.2 convert_element_type.8
  73.1 0.0 copy-done
  73.1 0.0 copy-start.1
  73.1 0.8 copy-done.1
  73.9 17.2 %decode.1 = bf16[4,240,384]{2,1,0:T(8,128)(2,1)S(1)} custom-call(f32[80,128]{1,0:T(8,128)S(1)} %copy-done.1, f32[16,40,128]{2,1,0:T(8,128)S(1)} %pad_convert_fusion.lat_ref, bf16[9,48,384]{2,1,0:T(8,128)(2,1)S(1)} %bitcast.5, bf16[3,3456,384]{2,1,0:T(8,128)(2,1)} %bitcast.6, f32[1,384]{1,0:T(1,128)S(1)} %reshape.21.gamma_ref), custom_call_target="tpu_custom_call" | custom-call | flops 5096079360 | bytes 10485760 | tf_op jit(solution)/shard_map/decode/pallas_call | solution.py:518
  91.1 1.0 %fusion = bf16[4,6,40,384]{3,2,1,0:T(8,128)(2,1)} fusion(s32[]{:T(128)S(6)} %select_n.17, bf16[4,6,40,384]{3,2,1,0:T(8,128)(2,1)S(1)} %bitcast.4, pred[6]{0:T(512)(128)(4,1)S(1)} %iota_compare_fusion), kind=kLoop, calls=%fused_computation.1 | loop fusion | flops 368640 | bytes 1474570 | tf_op jit(solution)/shard_map/jit(_where)/select_n | solution.py:567
  (1 shorter events, 0.0 us)
Async XLA Ops:
  3.3 69.6 %copy-start.2 = (bf16[4,4,640]{2,1,0:T(4,128)(2,1)S(1)}, bf16[4,4,640]{2,1,0:T(4,128)(2,1)}, u32[]{:S(2)}) copy-start(bf16[4,4,640]{2,1,0:T(4,128)(2,1)} %param.12) | copy-start | bytes 61444
  3.3 69.8 %copy-start = (bf16[3,3,3,16,384]{4,3,2,1,0:T(8,128)(2,1)S(1)}, bf16[3,3,3,16,384]{4,3,2,1,0:T(8,128)(2,1)}, u32[]{:S(2)}) copy-start(bf16[3,3,3,16,384]{4,3,2,1,0:T(8,128)(2,1)} %param.15) | copy-start | bytes 995332
  73.1 0.8 copy-start.1

commit v3 on v2

--- a/solution.py
+++ b/solution.py
@@ -28,8 +28,8 @@
 V_AFTER = 1
 
 CHIPS = (
-    (0, 0), (1, 0), (3, 0), (0, 1), (0, 3), (1, 1), (3, 3), (1, 3),
-    (3, 1), (2, 0), (0, 2), (2, 1), (1, 2), (2, 3), (3, 2), (2, 2),
+    (0, 0), (1, 1), (3, 3), (2, 2), (1, 3), (3, 1), (2, 0), (0, 2),
+    (1, 0), (3, 2), (0, 1), (2, 3), (3, 0), (1, 2), (0, 3), (2, 1),
 )
 ARRIVE = ("K0", "Q0", "Q1", "Q2", "Q3", "K1", "Q4", "Q5", "K2", "K3", "Q6", "Q7")
 
@@ -76,11 +76,14 @@
     return look
 
 
-def attend_kernel(
-    q_hbm, k_hbm, v_hbm, w_hbm, out_ref,
+def clip_kernel(
+    q_hbm, k_hbm, v_hbm, w_hbm, lat_hbm, first_hbm, mid_hbm, gamma_ref, band_ref, out_ref,
     v_in, w_in, v_send, q_got, k_got, v_got, q2, k2, v2, acc_ref, top_ref, s_ref, tile_top,
     y_send, y_got, in_sem, send_sem, q_sem, k_sem, v_sem, y_sem,
+    lat_in, lat, w_first, turned, win, own, above, below, near, first_in, w1, first, wide, taps,
+    total, w2, mine, extra, halo_ssem, halo_rsem, pair_sem,
 ):
+    bf16, f32 = jnp.bfloat16, jnp.float32
     me = lax.axis_index("seq")
     my_x, my_z, my_c = me // 8, lax.rem(me // 2, 4), lax.rem(me, 2)
     look_dx = packed_table([c[0] for c in CHIPS], 2)
@@ -172,6 +175,37 @@
                 pltpu.make_async_copy(v_send.at[0], v_got.at[0], v_sem.at[0]).start()
             pending = []
 
+    lat_load = pltpu.make_async_copy(lat_hbm, lat_in, in_sem.at[2])
+    first_load = pltpu.make_async_copy(first_hbm, w_first, in_sem.at[3])
+    mid_load = pltpu.make_async_copy(mid_hbm, w2, in_sem.at[4])
+    lat_load.start()
+    first_load.start()
+    mid_load.start()
+    win[...] = jnp.zeros_like(win)
+    wide[:, 0:8, :] = jnp.zeros((FRAMES * 6, 8, CH), f32)
+    wide[:, 48:56, :] = jnp.zeros((FRAMES * 6, 8, CH), f32)
+    own[:, LCOLS:, :] = jnp.zeros((4, 8, HEAD), f32)
+    blank = jnp.zeros((240, HEAD), bf16)
+    first_in[0, :, 0:128] = blank
+    first_in[0, :, 128:256] = blank
+    first_in[1, :, 0:128] = blank
+    first_in[0, :, 384:512] = blank
+    lat_load.wait()
+    flat = jnp.concatenate([lat_in[f].astype(f32) for f in range(FRAMES)], axis=0)
+    for block in range(5):
+        lanes = flat[:, block * HEAD:(block + 1) * HEAD]
+        for u in range(8):
+            x = block * 8 + u
+            lat[x * 16:(x + 1) * 16, :] = lanes if u == 0 else pltpu.roll(lanes, HEAD - LAT_CH * u, 1)
+    w1[...] = jnp.zeros_like(w1)
+    first_load.wait()
+    for s in range(3):
+        w1[s * HEAD:s * HEAD + 48, :] = w_first[s * 3]
+        w1[s * HEAD + 64:s * HEAD + 112, :] = w_first[s * 3 + 1]
+    w1[384:432, :] = w_first[2]
+    w1[448:496, :] = w_first[5]
+    w1[512:560, :] = w_first[8]
+
     def q_rows(i):
         return pl.ds(pl.multiple_of(i * QB, QB), QB)
 
@@ -297,78 +331,14 @@
     def gather(j, total):
         return total + y_got[j].astype(jnp.float32)
 
-    out_ref[...] = lax.fori_loop(1, SEQ, gather, y_send[0].astype(jnp.float32), unroll=True)
-    arrived(k_got.at[pl.ds(TOK, TOKENS - TOK)], send_sem.at[0])
-    arrived(q_got.at[pl.ds(TOK, TOKENS - TOK)], send_sem.at[1])
-    arrived(v_got.at[others], send_sem.at[2])
-    arrived(y_got.at[others], send_sem.at[3])
-
-
-def attend(query, key, value, head_weight):
-    bf16, f32 = jnp.bfloat16, jnp.float32
-    any_space = pl.BlockSpec(memory_space=pl.ANY)
-    return pl.pallas_call(
-        attend_kernel,
-        out_shape=jax.ShapeDtypeStruct((80, HEAD), f32),
-        in_specs=[any_space] * 4,
-        out_specs=pl.BlockSpec(memory_space=pltpu.VMEM),
-        scratch_shapes=[
-            pltpu.VMEM((TOK, HEADS * HEAD), bf16),
-            pltpu.VMEM((64, HEADS * HEAD), bf16),
-            pltpu.VMEM((SEQ, 80, HEAD), bf16),
-            pltpu.VMEM((TOKENS, HEAD), bf16),
-            pltpu.VMEM((TOKENS, HEAD), bf16),
-            pltpu.VMEM((SEQ, 80, HEAD), bf16),
-            pltpu.VMEM((TOKENS, 2 * HEAD), bf16),
-            pltpu.VMEM((TOKENS, 2 * HEAD), bf16),
-            pltpu.VMEM((TOKENS, HEAD), bf16),
-            pltpu.VMEM((TOKENS, HEAD), f32),
-            pltpu.VMEM((TOKENS, HEAD), f32),
-            pltpu.VMEM((2, QB, KB), f32),
-            pltpu.VMEM((2, QB, HEAD), f32),
-            pltpu.VMEM((SEQ, 80, HEAD), bf16),
-            pltpu.VMEM((SEQ, 80, HEAD), bf16),
-            pltpu.SemaphoreType.DMA((2,)),
-            pltpu.SemaphoreType.DMA((4,)),
-            pltpu.SemaphoreType.DMA((NQ,)),
-            pltpu.SemaphoreType.DMA((NK,)),
-            pltpu.SemaphoreType.DMA((NK,)),
-            pltpu.SemaphoreType.DMA,
-        ],
-        compiler_params=pltpu.CompilerParams(
-            collective_id=1, has_side_effects=True, vmem_limit_bytes=56 * 2**20
-        ),
-        cost_estimate=pl.CostEstimate(
-            flops=4 * TOKENS * TOKENS * HEAD, bytes_accessed=16 * 2**20,
-            transcendentals=TOKENS * TOKENS,
-        ),
-        name="attend",
-    )(query, key, value, head_weight.T)
-
-
-def decode_kernel(
-    vel_ref, lat_ref, w_first, w_mid, gamma_ref, out_ref,
-    turned, win, own, above, below, near, first_in, w1, first, wide, taps, total, w2, extra,
-    in_sem, halo_ssem, halo_rsem, pair_sem,
-):
-    me = lax.axis_index("seq")
+    vel = lax.fori_loop(1, SEQ, gather, y_send[0].astype(f32), unroll=True)
     up, down = lax.rem(me + SEQ - 1, SEQ), lax.rem(me + 1, SEQ)
     odd = lax.rem(me, 2)
-    bf16, f32 = jnp.bfloat16, jnp.float32
-    w_load = pltpu.make_async_copy(w_mid, w2, in_sem.at[0])
-    w_load.start()
-    barrier = pltpu.get_barrier_semaphore()
-    for to in (up, down):
-        pl.semaphore_signal(
-            barrier, inc=1, device_id={"seq": to}, device_id_type=pl.DeviceIdType.MESH
-        )
-
+    lane40 = lax.broadcasted_iota(jnp.int32, (LCOLS, HEAD), 1)
     lane20 = lax.broadcasted_iota(jnp.int32, (80, HEAD), 1)
-    vel = vel_ref[...]
     for o in range(8):
         turn = vel if o == 0 else pltpu.roll(vel, HEAD - LAT_CH * o, 1)
         turned[o] = jnp.where(lane20 < LAT_CH, turn, 0.0)
-    win[...] = jnp.zeros_like(win)
     for f in range(FRAMES):
         for r in range(BAND):
             for a in range(2):
@@ -378,18 +348,17 @@
                     win[row, pl.ds(8 + b, PCOLS, stride=2), :] = turned[
                         o, pl.ds(((f % 2) * BAND + r) * PCOLS, PCOLS), :
                     ]
-    own[:, LCOLS:, :] = jnp.zeros((4, 8, HEAD), f32)
     for y in range(4):
         merged = jnp.zeros((LCOLS, HEAD), f32)
         for f in range(FRAMES):
             grid = win[f * 8 + 2 + y, 8:48, :]
-            clean = (lat_ref[f * 4 + y] - 0.9 * grid).astype(bf16).astype(f32)
+            clean = (lat[pl.ds(f * 4 + y, LCOLS, stride=16), :] - 0.9 * grid).astype(bf16).astype(f32)
+            clean = jnp.where(lane40 < LAT_CH, clean, 0.0)
             win[f * 8 + 2 + y, 8:48, :] = clean
             merged = merged + (clean if f == 0 else pltpu.roll(clean, LAT_CH * f, 1))
         own[y, 0:LCOLS, :] = merged
     near[0] = own[0:2].astype(bf16)
     near[1] = own[2:4].astype(bf16)
-    pl.semaphore_wait(barrier, 2)
     to_up = pltpu.make_async_remote_copy(
         src_ref=near.at[0], dst_ref=below, send_sem=halo_ssem.at[0], recv_sem=halo_rsem.at[0],
         device_id={"seq": up}, device_id_type=pl.DeviceIdType.MESH,
@@ -401,19 +370,8 @@
     to_up.start()
     to_down.start()
 
-    w1[...] = jnp.zeros_like(w1)
-    for s in range(3):
-        w1[s * HEAD:s * HEAD + 48, :] = w_first[s * 3]
-        w1[s * HEAD + 64:s * HEAD + 112, :] = w_first[s * 3 + 1]
-    w1[384:432, :] = w_first[2]
-    w1[448:496, :] = w_first[5]
-    w1[512:560, :] = w_first[8]
-    wide[:, 0:8, :] = jnp.zeros((FRAMES * 6, 8, CH), f32)
-    wide[:, 48:56, :] = jnp.zeros((FRAMES * 6, 8, CH), f32)
-
     to_up.wait_recv()
     to_down.wait_recv()
-    lane40 = lax.broadcasted_iota(jnp.int32, (LCOLS, HEAD), 1)
     for side in range(2):
         there = (me > 0) if side == 0 else (me < SEQ - 1)
         got = above if side == 0 else below
@@ -448,11 +406,6 @@
         return carry
 
     lax.fori_loop(0, FRAMES, gather_columns, 0)
-    blank = jnp.zeros((240, HEAD), bf16)
-    first_in[0, :, 0:128] = blank
-    first_in[0, :, 128:256] = blank
-    first_in[1, :, 0:128] = blank
-    first_in[0, :, 384:512] = blank
     first_in[1, :, 384:512] = pltpu.roll(total[0], 64, 1).astype(bf16)
     first_in[2, :, 384:512] = (total[0] + pltpu.roll(total[1], 64, 1)).astype(bf16)
     first_in[3, :, 384:512] = (total[1] + pltpu.roll(total[2], 64, 1)).astype(bf16)
@@ -477,7 +430,7 @@
         return carry
 
     lax.fori_loop(0, FRAMES, first_step, 0)
-    w_load.wait()
+    mid_load.wait()
     for s in (2, 1, 0):
         count = FRAMES - (2 - s)
         for part in range(3):
@@ -488,9 +441,9 @@
             ).reshape(count, TOK, CH)
             first[2 - s:FRAMES] = first[2 - s:FRAMES] + term
 
-    out_ref[:, 0:TOK, :] = first[...].astype(bf16)
+    mine[...] = first[...].astype(bf16)
     hand = pltpu.make_async_remote_copy(
-        src_ref=out_ref.at[:, pl.ds(0, 80), :], dst_ref=extra,
+        src_ref=mine.at[:, pl.ds(0, 80), :], dst_ref=extra,
         send_sem=pair_sem.at[0], recv_sem=pair_sem.at[1],
         device_id={"seq": me - odd}, device_id_type=pl.DeviceIdType.MESH,
     )
@@ -498,29 +451,75 @@
     @pl.when(odd == 1)
     def _():
         hand.start()
+
+    length = band_ref[me]
+    lead = odd * (2 * BAND - length)
+    for f in range(FRAMES):
+        for i in range(4):
+            row = first[f, i * LCOLS:(i + 1) * LCOLS, :]
+            for later in (1, 2):
+                if i + later < 4:
+                    at = (i + later) * LCOLS
+                    row = jnp.where(lead == later, first[f, at:at + LCOLS, :], row)
+            row = jnp.where(i < length, row, 0.0)
+            out_ref[f, i * LCOLS:(i + 1) * LCOLS, :] = row.astype(bf16)
+
+    @pl.when(odd == 1)
+    def _():
         hand.wait_send()
         out_ref[:, TOK:TOK + 80, :] = jnp.zeros((FRAMES, 80, CH), bf16)
 
     @pl.when(odd == 0)
     def _():
         hand.wait_recv()
-        out_ref[:, TOK:TOK + 80, :] = extra[...]
+        for f in range(FRAMES):
+            got = extra[f].astype(f32)
+            place = lax.broadcasted_iota(jnp.int32, (80, CH), 0)
+            got = jnp.where(place < (length - 4) * LCOLS, got, 0.0)
+            out_ref[f, TOK:TOK + 80, :] = got.astype(bf16)
 
     to_up.wait_send()
     to_down.wait_send()
-
-
-def decode(velocity, latent, conv_in, conv_mid, gamma):
+    arrived(k_got.at[pl.ds(TOK, TOKENS - TOK)], send_sem.at[0])
+    arrived(q_got.at[pl.ds(TOK, TOKENS - TOK)], send_sem.at[1])
+    arrived(v_got.at[others], send_sem.at[2])
+    arrived(y_got.at[others], send_sem.at[3])
+
+
+def decode_clip(query, key, value, latent, band_rows, head_weight, conv_in, conv_mid, gamma):
     bf16, f32 = jnp.bfloat16, jnp.float32
+    any_space = pl.BlockSpec(memory_space=pl.ANY)
     vmem = pl.BlockSpec(memory_space=pltpu.VMEM)
-    spaced = latent.reshape(FRAMES * 4, LCOLS, LAT_CH).astype(f32)
-    spaced = jnp.pad(spaced, ((0, 0), (0, 0), (0, HEAD - LAT_CH)))
     return pl.pallas_call(
-        decode_kernel,
+        clip_kernel,
         out_shape=jax.ShapeDtypeStruct((FRAMES, TOK + 80, CH), bf16),
-        in_specs=[vmem, vmem, vmem, pl.BlockSpec(memory_space=pl.ANY), vmem],
+        in_specs=[any_space] * 7 + [vmem, pl.BlockSpec(memory_space=pltpu.SMEM)],
         out_specs=vmem,
         scratch_shapes=[
+            pltpu.VMEM((TOK, HEADS * HEAD), bf16),
+            pltpu.VMEM((64, HEADS * HEAD), bf16),
+            pltpu.VMEM((SEQ, 80, HEAD), bf16),
+            pltpu.VMEM((TOKENS, HEAD), bf16),
+            pltpu.VMEM((TOKENS, HEAD), bf16),
+            pltpu.VMEM((SEQ, 80, HEAD), bf16),
+            pltpu.VMEM((TOKENS, 2 * HEAD), bf16),
+            pltpu.VMEM((TOKENS, 2 * HEAD), bf16),
+            pltpu.VMEM((TOKENS, HEAD), bf16),
+            pltpu.VMEM((TOKENS, HEAD), f32),
+            pltpu.VMEM((TOKENS, HEAD), f32),
+            pltpu.VMEM((2, QB, KB), f32),
+            pltpu.VMEM((2, QB, HEAD), f32),
+            pltpu.VMEM((SEQ, 80, HEAD), bf16),
+            pltpu.VMEM((SEQ, 80, HEAD), bf16),
+            pltpu.SemaphoreType.DMA((5,)),
+            pltpu.SemaphoreType.DMA((4,)),
+            pltpu.SemaphoreType.DMA((NQ,)),
+            pltpu.SemaphoreType.DMA((NK,)),
+            pltpu.SemaphoreType.DMA((NK,)),
+            pltpu.SemaphoreType.DMA,
+            pltpu.VMEM((FRAMES, 4, LCOLS * LAT_CH), bf16),
+            pltpu.VMEM((LCOLS * 16, HEAD), f32),
+            pltpu.VMEM((9, 48, CH), bf16),
             pltpu.VMEM((8, 80, HEAD), f32),
             pltpu.VMEM((FRAMES * 8, 56, HEAD), f32),
             pltpu.VMEM((4, 48, HEAD), f32),
@@ -534,37 +533,31 @@
             pltpu.VMEM((FRAMES, TOK, 9 * CH), bf16),
             pltpu.VMEM((FRAMES, 240, HEAD), f32),
             pltpu.VMEM((3, 9 * CH, CH), bf16),
+            pltpu.VMEM((FRAMES, TOK, CH), bf16),
             pltpu.VMEM((FRAMES, 80, CH), bf16),
-            pltpu.SemaphoreType.DMA((1,)),
             pltpu.SemaphoreType.DMA((2,)),
             pltpu.SemaphoreType.DMA((2,)),
             pltpu.SemaphoreType.DMA((2,)),
         ],
         compiler_params=pltpu.CompilerParams(
-            collective_id=2, has_side_effects=True, vmem_limit_bytes=48 * 2**20
+            collective_id=1, has_side_effects=True, vmem_limit_bytes=58 * 2**20
         ),
         cost_estimate=pl.CostEstimate(
-            flops=2 * 640 * 27 * CH * CH, bytes_accessed=10 * 2**20, transcendentals=960 * CH
+            flops=4 * TOKENS * TOKENS * HEAD, bytes_accessed=24 * 2**20,
+            transcendentals=TOKENS * TOKENS,
         ),
-        name="decode",
+        name="clip",
     )(
-        velocity, spaced, conv_in.reshape(9, 48, CH), conv_mid.reshape(3, 9 * CH, CH),
-        gamma.reshape(1, CH),
+        query, key, value, head_weight.T, latent, conv_in.reshape(9, 48, CH),
+        conv_mid.reshape(3, 9 * CH, CH), gamma.reshape(1, CH), band_rows,
     )
 
 
 def per_device(query, key, value, latent, band_rows, head_weight, conv_in, conv_mid, gamma):
-    place = lax.axis_index("seq")
-    velocity = attend(query, key, value, head_weight)
-    decoded = decode(velocity, latent, conv_in, conv_mid, gamma)
-    decoded = decoded.reshape(FRAMES, 3 * BAND, LCOLS, CH)
-    groups = lax.axis_size("seq")
-    length = jnp.sum(jnp.where(jnp.arange(groups, dtype=jnp.int32) == place, band_rows, 0))
-    lead = jnp.where(lax.rem(place, 2) == 1, 2 * BAND - length, 0)
-    extended = jnp.pad(decoded, ((0, 0), (0, BAND), (0, 0), (0, 0)))
-    picked = lax.dynamic_slice_in_dim(extended, lead, 3 * BAND, 1)
-    keep_mask = jnp.arange(3 * BAND, dtype=jnp.int32) < length
-    return jnp.where(keep_mask[None, :, None, None], picked, jnp.zeros_like(picked))
+    rows = decode_clip(
+        query, key, value, latent, band_rows, head_weight, conv_in, conv_mid, gamma
+    )
+    return rows.reshape(FRAMES, 3 * BAND, LCOLS, CH)
 
 
 def solution(mesh):

time: 93.4 us -> 90.1 us (0.965); the launches traced: 92.2 us -> 89.9 us
  other arithmetic: 3 us -> 0 us
  local copies, waits for them, and re-layouts: 1.65 us -> 3.3 us
    reduce_sum x1 -> x0, other arithmetic: 1.29 us -> none  [per_device(): jnp.sum(jnp.where(jnp.arange(groups, dtype=jnp.int32) == place, band_rows...]
    unnamed x6 -> x1, local copies, waits for them, and re-layouts: 0.78 us -> 2.05 us
    select_n x1 -> x0, other arithmetic: 1.03 us -> none  [per_device(): jnp.where(keep_mask[None, :, None, None], picked, jnp.zeros_like(picked))]
    pallas_call x2 -> x1, Pallas kernels: 86.8 us -> 86.6 us  [decode_clip(): pl.pallas_call(clip_kernel, out_shape=jax.ShapeDtypeStruct((FRAMES, TOK +...]
where the time goes in v3:
time: 90.1 us; the launch traced here: 89.9 us
  Pallas kernels  86.6 us (96%)
  local copies, waits for them, and re-layouts  3.3 us (4%)
    pallas_call x1, Pallas kernels, decode_clip(): pl.pallas_call(clip_kernel, out_shape=jax.ShapeDtypeStruct((FRAMES, TOK +...  86.6 us
    unnamed x1, local copies, waits for them, and re-layouts  2.05 us

profile of v3, /device:TPU:0, one launch (start us, length us, event | category | flops | bytes accessed | tf_op | source)
XLA Modules:
  0.0 89.9 jit_solution(390334303420150442)
XLA Ops:
  0.0 1.2 %reshape.14.gamma_ref = f32[1,384]{1,0:T(1,128)} reshape(f32[384]{0:T(512)} %param.17) | data formatting | bytes 3072 | tf_op jit(solution)/shard_map/reshape | solution.py:552
  1.2 86.6 %clip.1 = bf16[4,240,384]{2,1,0:T(8,128)(2,1)} custom-call(bf16[160,4096]{1,0:T(8,128)(2,1)} %q_hbm.1, bf16[160,4096]{1,0:T(8,128)(2,1)} %k_hbm.1, bf16[160,4096]{1,0:T(8,128)(2,1)} %v_hbm.1, bf16[64,4096]{1,0:T(8,128)(2,1)} %bitcast.6, bf16[4,4,640]{2,1,0:T(4,128)(2,1)} %lat_hbm.1, bf16[9,48,384]{2,1,0:T(8,128)(2,1)} %bitcast.7, ...), custom_call_target="tpu_custom_call" | custom-call | flops 13421772800 | bytes 25165824 | tf_op jit(solution)/shard_map/clip/pallas_call | solution.py:493
  87.8 2.1 %copy.11 = bf16[4,6,40,384]{3,2,1,0:T(8,128)(2,1)} copy(bf16[4,6,40,384]{3,2,1,0:T(8,128)(2,1)} %bitcast.4) | data formatting | bytes 1474560

commit v4 on v3

--- a/solution.py
+++ b/solution.py
@@ -26,12 +26,13 @@
 SCALE = math.log2(math.e) / math.sqrt(HEAD)
 NEG = -1e30
 V_AFTER = 1
+MID_AT = 14
 
 CHIPS = (
     (0, 0), (1, 1), (3, 3), (2, 2), (1, 3), (3, 1), (2, 0), (0, 2),
     (1, 0), (3, 2), (0, 1), (2, 3), (3, 0), (1, 2), (0, 3), (2, 1),
 )
-ARRIVE = ("K0", "Q0", "Q1", "Q2", "Q3", "K1", "Q4", "Q5", "K2", "K3", "Q6", "Q7")
+ARRIVE = ("K0", "Q0", "Q1", "K1", "Q2", "Q3", "Q4", "K2", "Q5", "Q6", "K3", "Q7")
 
 
 def plan_tiles():
@@ -77,11 +78,12 @@
 
 
 def clip_kernel(
-    q_hbm, k_hbm, v_hbm, w_hbm, lat_hbm, first_hbm, mid_hbm, gamma_ref, band_ref, out_ref,
+    q_hbm, k_hbm, v_hbm, w_hbm, lat_hbm, first_hbm, mid_hbm, gamma_hbm, band_hbm, out_ref,
     v_in, w_in, v_send, q_got, k_got, v_got, q2, k2, v2, acc_ref, top_ref, s_ref, tile_top,
     y_send, y_got, in_sem, send_sem, q_sem, k_sem, v_sem, y_sem,
     lat_in, lat, w_first, turned, win, own, above, below, near, first_in, w1, first, wide, taps,
     total, w2, mine, extra, halo_ssem, halo_rsem, pair_sem,
+    gamma_in, band_in,
 ):
     bf16, f32 = jnp.bfloat16, jnp.float32
     me = lax.axis_index("seq")
@@ -178,9 +180,12 @@
     lat_load = pltpu.make_async_copy(lat_hbm, lat_in, in_sem.at[2])
     first_load = pltpu.make_async_copy(first_hbm, w_first, in_sem.at[3])
     mid_load = pltpu.make_async_copy(mid_hbm, w2, in_sem.at[4])
+    gamma_load = pltpu.make_async_copy(gamma_hbm, gamma_in, in_sem.at[5])
+    band_load = pltpu.make_async_copy(band_hbm, band_in, in_sem.at[6])
     lat_load.start()
     first_load.start()
-    mid_load.start()
+    gamma_load.start()
+    band_load.start()
     win[...] = jnp.zeros_like(win)
     wide[:, 0:8, :] = jnp.zeros((FRAMES * 6, 8, CH), f32)
     wide[:, 48:56, :] = jnp.zeros((FRAMES * 6, 8, CH), f32)
@@ -197,6 +202,8 @@
         for u in range(8):
             x = block * 8 + u
             lat[x * 16:(x + 1) * 16, :] = lanes if u == 0 else pltpu.roll(lanes, HEAD - LAT_CH * u, 1)
+    gamma_load.wait()
+    band_load.wait()
     w1[...] = jnp.zeros_like(w1)
     first_load.wait()
     for s in range(3):
@@ -302,6 +309,10 @@
         )
 
     def after(t):
+        @pl.when(t == MID_AT)
+        def _():
+            mid_load.start()
+
         @pl.when(look_last(t) == 1)
         def _():
             finish(look_q(t))
@@ -414,7 +425,7 @@
         conv = jnp.dot(first_in[f], w1[...], preferred_element_type=f32)
         values = conv.astype(bf16).astype(f32)
         power = jnp.mean(values * values, axis=1, keepdims=True)
-        normed = values * lax.rsqrt(power + 1e-06) * gamma_ref[...]
+        normed = values * lax.rsqrt(power + 1e-06) * gamma_in[...].reshape(1, CH)
         normed = normed / (1.0 + jnp.exp(-normed))
         place = lax.broadcasted_iota(jnp.int32, (240, CH), 0)
         outside = ((place < 40) & (me == 0)) | ((place >= 200) & (me == SEQ - 1))
@@ -452,7 +463,7 @@
     def _():
         hand.start()
 
-    length = band_ref[me]
+    length = band_in[me]
     lead = odd * (2 * BAND - length)
     for f in range(FRAMES):
         for i in range(4):
@@ -488,12 +499,12 @@
 
 def decode_clip(query, key, value, latent, band_rows, head_weight, conv_in, conv_mid, gamma):
     bf16, f32 = jnp.bfloat16, jnp.float32
-    any_space = pl.BlockSpec(memory_space=pl.ANY)
+    any_space = pl.BlockSpec(memory_space=pltpu.HBM)
     vmem = pl.BlockSpec(memory_space=pltpu.VMEM)
     return pl.pallas_call(
         clip_kernel,
         out_shape=jax.ShapeDtypeStruct((FRAMES, TOK + 80, CH), bf16),
-        in_specs=[any_space] * 7 + [vmem, pl.BlockSpec(memory_space=pltpu.SMEM)],
+        in_specs=[any_space] * 9,
         out_specs=vmem,
         scratch_shapes=[
             pltpu.VMEM((TOK, HEADS * HEAD), bf16),
@@ -511,7 +522,7 @@
             pltpu.VMEM((2, QB, HEAD), f32),
             pltpu.VMEM((SEQ, 80, HEAD), bf16),
             pltpu.VMEM((SEQ, 80, HEAD), bf16),
-            pltpu.SemaphoreType.DMA((5,)),
+            pltpu.SemaphoreType.DMA((7,)),
             pltpu.SemaphoreType.DMA((4,)),
             pltpu.SemaphoreType.DMA((NQ,)),
             pltpu.SemaphoreType.DMA((NK,)),
@@ -538,9 +549,11 @@
             pltpu.SemaphoreType.DMA((2,)),
             pltpu.SemaphoreType.DMA((2,)),
             pltpu.SemaphoreType.DMA((2,)),
+            pltpu.VMEM((CH,), f32),
+            pltpu.SMEM((SEQ,), jnp.int32),
         ],
         compiler_params=pltpu.CompilerParams(
-            collective_id=1, has_side_effects=True, vmem_limit_bytes=58 * 2**20
+            collective_id=1, has_side_effects=True, vmem_limit_bytes=56 * 2**20
         ),
         cost_estimate=pl.CostEstimate(
             flops=4 * TOKENS * TOKENS * HEAD, bytes_accessed=24 * 2**20,
@@ -549,7 +562,7 @@
         name="clip",
     )(
         query, key, value, head_weight.T, latent, conv_in.reshape(9, 48, CH),
-        conv_mid.reshape(3, 9 * CH, CH), gamma.reshape(1, CH), band_rows,
+        conv_mid.reshape(3, 9 * CH, CH), gamma, band_rows,
     )
 
 

time: 90.1 us -> 86.9 us (0.964)
  Pallas kernels: 86.6 us -> 84.7 us
  local copies, waits for them, and re-layouts: 3.3 us -> 2.05 us
    pallas_call x1, Pallas kernels: 86.6 us -> 84.7 us  [decode_clip(): pl.pallas_call(clip_kernel, out_shape=jax.ShapeDtypeStruct((FRAMES, TOK +...]
    reshape x1 -> x0, local copies, waits for them, and re-layouts: 1.24 us -> none  [decode_clip(): gamma.reshape(1, CH)]
where the time goes in v4:
time: 86.9 us; the launch traced here: 86.8 us
  Pallas kernels  84.7 us (97%)
  local copies, waits for them, and re-layouts  2.05 us (2%)
    pallas_call x1, Pallas kernels, decode_clip(): pl.pallas_call(clip_kernel, out_shape=jax.ShapeDtypeStruct((FRAMES, TOK +...  84.7 us
    unnamed x1, local copies, waits for them, and re-layouts  2.05 us

profile of v4, /device:TPU:0, one launch (start us, length us, event | category | flops | bytes accessed | tf_op | source)
XLA Modules:
  0.0 86.8 jit_solution(18136849389415350564)
XLA Ops:
  0.0 84.7 %clip.1 = bf16[4,240,384]{2,1,0:T(8,128)(2,1)} custom-call(bf16[160,4096]{1,0:T(8,128)(2,1)} %q_hbm.1, bf16[160,4096]{1,0:T(8,128)(2,1)} %k_hbm.1, bf16[160,4096]{1,0:T(8,128)(2,1)} %v_hbm.1, bf16[64,4096]{1,0:T(8,128)(2,1)} %bitcast.6, bf16[4,4,640]{2,1,0:T(4,128)(2,1)} %lat_hbm.1, bf16[9,48,384]{2,1,0:T(8,128)(2,1)} %bitcast.7, ...), custom_call_target="tpu_custom_call" | custom-call | flops 13421772800 | bytes 25165824 | tf_op jit(solution)/shard_map/clip/pallas_call | solution.py:504
  84.7 2.1 %copy.11 = bf16[4,6,40,384]{3,2,1,0:T(8,128)(2,1)} copy(bf16[4,6,40,384]{3,2,1,0:T(8,128)(2,1)} %bitcast.4) | data formatting | bytes 1474560

commit v5 on v4

--- a/solution.py
+++ b/solution.py
@@ -82,7 +82,7 @@
     v_in, w_in, v_send, q_got, k_got, v_got, q2, k2, v2, acc_ref, top_ref, s_ref, tile_top,
     y_send, y_got, in_sem, send_sem, q_sem, k_sem, v_sem, y_sem,
     lat_in, lat, w_first, turned, win, own, above, below, near, first_in, w1, first, wide, taps,
-    total, w2, mine, extra, halo_ssem, halo_rsem, pair_sem,
+    total, w2, w3, w4, mine, extra, halo_ssem, halo_rsem, pair_sem,
     gamma_in, band_in,
 ):
     bf16, f32 = jnp.bfloat16, jnp.float32
@@ -118,21 +118,21 @@
     def arrived(ref, sem):
         pltpu.make_async_copy(ref, ref, sem).wait()
 
+    barrier = pltpu.get_barrier_semaphore()
+
+    def greet(j, carry):
+        pl.semaphore_signal(
+            barrier, inc=1, device_id={"seq": ahead(j)}, device_id_type=pl.DeviceIdType.MESH
+        )
+        return carry
+
+    lax.fori_loop(1, SEQ, greet, 0, unroll=True)
     v_load = pltpu.make_async_copy(v_hbm, v_in, in_sem.at[0])
     w_load = pltpu.make_async_copy(w_hbm, w_in, in_sem.at[1])
     v_load.start()
     w_load.start()
     pltpu.make_async_copy(k_hbm.at[:, head_cols(me)], k_got.at[pl.ds(0, TOK)], k_sem.at[0]).start()
     pltpu.make_async_copy(q_hbm.at[:, head_cols(me)], q_got.at[pl.ds(0, TOK)], q_sem.at[0]).start()
-    barrier = pltpu.get_barrier_semaphore()
-
-    def greet(j, carry):
-        pl.semaphore_signal(
-            barrier, inc=1, device_id={"seq": ahead(j)}, device_id_type=pl.DeviceIdType.MESH
-        )
-        return carry
-
-    lax.fori_loop(1, SEQ, greet, 0)
     pl.semaphore_wait(barrier, SEQ - 1)
 
     def send_k(j, carry):
@@ -162,10 +162,10 @@
     for at, name in enumerate(ARRIVE):
         place = int(name[1])
         if name[0] == "K":
-            lax.fori_loop(max(1, place * 8), place * 8 + 8, send_k, 0)
+            lax.fori_loop(max(1, place * 8), place * 8 + 8, send_k, 0, unroll=True)
             pending.append(place)
         else:
-            lax.fori_loop(max(1, place * 4), place * 4 + 4, send_q, 0)
+            lax.fori_loop(max(1, place * 4), place * 4 + 4, send_q, 0, unroll=True)
         if at >= V_AFTER and pending:
             if pending[0] == 0:
                 v_load.wait()
@@ -179,9 +179,18 @@
 
     lat_load = pltpu.make_async_copy(lat_hbm, lat_in, in_sem.at[2])
     first_load = pltpu.make_async_copy(first_hbm, w_first, in_sem.at[3])
-    mid_load = pltpu.make_async_copy(mid_hbm, w2, in_sem.at[4])
-    gamma_load = pltpu.make_async_copy(gamma_hbm, gamma_in, in_sem.at[5])
-    band_load = pltpu.make_async_copy(band_hbm, band_in, in_sem.at[6])
+    last = pl.ds(256, HEAD)
+    mid_loads = [
+        pltpu.make_async_copy(source, target, in_sem.at[4 + n])
+        for n, (source, target) in enumerate((
+            (mid_hbm.at[:, :, pl.ds(0, 256)], w2),
+            (mid_hbm.at[2, :, last], w3.at[:, pl.ds(0, HEAD)]),
+            (mid_hbm.at[1, :, last], w3.at[:, pl.ds(HEAD, HEAD)]),
+            (mid_hbm.at[0, :, last], w4),
+        ))
+    ]
+    gamma_load = pltpu.make_async_copy(gamma_hbm, gamma_in, in_sem.at[8])
+    band_load = pltpu.make_async_copy(band_hbm, band_in, in_sem.at[9])
     lat_load.start()
     first_load.start()
     gamma_load.start()
@@ -311,7 +320,8 @@
     def after(t):
         @pl.when(t == MID_AT)
         def _():
-            mid_load.start()
+            for load in mid_loads:
+                load.start()
 
         @pl.when(look_last(t) == 1)
         def _():
@@ -441,17 +451,22 @@
         return carry
 
     lax.fori_loop(0, FRAMES, first_step, 0)
-    mid_load.wait()
+    for load in mid_loads:
+        load.wait()
+
+    def product(count, weights):
+        source = taps[0:count].reshape(count * TOK, 9 * CH)
+        return sum(
+            jnp.dot(source[:, low:high], weights[low:high, :], preferred_element_type=f32)
+            for low, high in ((0, 1280), (1280, 2560), (2560, 3456))
+        ).reshape(count, TOK, -1)
+
     for s in (2, 1, 0):
-        count = FRAMES - (2 - s)
-        for part in range(3):
-            cols = slice(part * 3 * CH, (part + 1) * 3 * CH)
-            term = jnp.dot(
-                taps[0:count, :, cols].reshape(count * TOK, 3 * CH), w2[s, cols, :],
-                preferred_element_type=f32,
-            ).reshape(count, TOK, CH)
-            first[2 - s:FRAMES] = first[2 - s:FRAMES] + term
-
+        first[2 - s:FRAMES, :, 0:256] = first[2 - s:FRAMES, :, 0:256] + product(2 + s, w2.at[s])
+    term = product(FRAMES, w3)
+    first[:, :, 256:CH] = first[:, :, 256:CH] + term[:, :, 0:HEAD]
+    first[1:FRAMES, :, 256:CH] = first[1:FRAMES, :, 256:CH] + term[0:FRAMES - 1, :, HEAD:]
+    first[2:FRAMES, :, 256:CH] = first[2:FRAMES, :, 256:CH] + product(2, w4)
     mine[...] = first[...].astype(bf16)
     hand = pltpu.make_async_remote_copy(
         src_ref=mine.at[:, pl.ds(0, 80), :], dst_ref=extra,
@@ -522,7 +537,7 @@
             pltpu.VMEM((2, QB, HEAD), f32),
             pltpu.VMEM((SEQ, 80, HEAD), bf16),
             pltpu.VMEM((SEQ, 80, HEAD), bf16),
-            pltpu.SemaphoreType.DMA((7,)),
+            pltpu.SemaphoreType.DMA((10,)),
             pltpu.SemaphoreType.DMA((4,)),
             pltpu.SemaphoreType.DMA((NQ,)),
             pltpu.SemaphoreType.DMA((NK,)),
@@ -543,7 +558,9 @@
             pltpu.VMEM((FRAMES * 6, 56, CH), f32),
             pltpu.VMEM((FRAMES, TOK, 9 * CH), bf16),
             pltpu.VMEM((FRAMES, 240, HEAD), f32),
-            pltpu.VMEM((3, 9 * CH, CH), bf16),
+            pltpu.VMEM((3, 9 * CH, 256), bf16),
+            pltpu.VMEM((9 * CH, 256), bf16),
+            pltpu.VMEM((9 * CH, HEAD), bf16),
             pltpu.VMEM((FRAMES, TOK, CH), bf16),
             pltpu.VMEM((FRAMES, 80, CH), bf16),
             pltpu.SemaphoreType.DMA((2,)),
@@ -566,11 +583,27 @@
     )
 
 
+def hand_out_kernel(rows_ref, out_ref):
+    out_ref[...] = rows_ref[...]
+
+
+def hand_out(rows):
+    frame = pl.BlockSpec((2,) + rows.shape[1:], lambda f: (f, 0, 0))
+    return pl.pallas_call(
+        hand_out_kernel,
+        grid=(2,),
+        out_shape=jax.ShapeDtypeStruct(rows.shape, rows.dtype),
+        in_specs=[frame],
+        out_specs=frame,
+        name="hand_out",
+    )(rows)
+
+
 def per_device(query, key, value, latent, band_rows, head_weight, conv_in, conv_mid, gamma):
     rows = decode_clip(
         query, key, value, latent, band_rows, head_weight, conv_in, conv_mid, gamma
     )
-    return rows.reshape(FRAMES, 3 * BAND, LCOLS, CH)
+    return hand_out(rows).reshape(FRAMES, 3 * BAND, LCOLS, CH)
 
 
 def solution(mesh):

time: 86.9 us -> 84.8 us (0.976)
  local copies, waits for them, and re-layouts: 2.05 us -> 0 us
    unnamed x1 -> x0, local copies, waits for them, and re-layouts: 2.05 us -> none
    pallas_call x1, Pallas kernels: 84.7 us -> 82.8 us  [decode_clip(): pl.pallas_call(clip_kernel, out_shape=jax.ShapeDtypeStruct((FRAMES, TOK +...]
    pallas_call x0 -> x1, Pallas kernels: none -> 1.89 us  [hand_out(): pl.pallas_call(hand_out_kernel, grid=(2,), out_shape=jax.ShapeDtypeStruct...]
where the time goes in v5:
time: 84.8 us; the launch traced here: 84.7 us
  Pallas kernels  84.7 us (100%)
    pallas_call x1, Pallas kernels, decode_clip(): pl.pallas_call(clip_kernel, out_shape=jax.ShapeDtypeStruct((FRAMES, TOK +...  82.8 us
    pallas_call x1, Pallas kernels, hand_out(): pl.pallas_call(hand_out_kernel, grid=(2,), out_shape=jax.ShapeDtypeStruct...  1.89 us

profile of v5, /device:TPU:0, one launch (start us, length us, event | category | flops | bytes accessed | tf_op | source)
XLA Modules:
  0.0 84.7 jit_solution(10993912370543819039)
XLA Ops:
  0.0 82.8 %clip.1.rows_ref = bf16[4,240,384]{2,1,0:T(8,128)(2,1)} custom-call(bf16[160,4096]{1,0:T(8,128)(2,1)} %q_hbm.1, bf16[160,4096]{1,0:T(8,128)(2,1)} %k_hbm.1, bf16[160,4096]{1,0:T(8,128)(2,1)} %v_hbm.1, bf16[64,4096]{1,0:T(8,128)(2,1)} %bitcast.5, bf16[4,4,640]{2,1,0:T(4,128)(2,1)} %lat_hbm.1, bf16[9,48,384]{2,1,0:T(8,128)(2,1)} %bitcast.6, ...), custom_call_target="tpu_custom_call" | custom-call | flops 13421772800 | bytes 25165824 | tf_op jit(solution)/shard_map/clip/pallas_call | solution.py:519
  82.8 1.9 %hand_out.1 = bf16[4,240,384]{2,1,0:T(8,128)(2,1)} custom-call(bf16[4,240,384]{2,1,0:T(8,128)(2,1)} %clip.1.rows_ref), custom_call_target="tpu_custom_call" | custom-call | tf_op jit(solution)/shard_map/hand_out/pallas_call | solution.py:592
